TPU v7x, 32 devices: a whole 2x2x4 slice. The times are simulated.
32 devices in a mesh: row: 4 (over z), col: 8 (over y, x, core).
Axes of the slice: x: 2, y: 2, z: 4, core: 2. Of those that a mesh axis runs over, the one named last changes fastest.
Arguments:
- singles: bfloat16 [512, 384], P('row', 'col'), may hold values from -6 to 6
- pair_in: bfloat16 [512, 512, 128], P('row', 'col'), may hold values from -6 to 6
- proj_weight: bfloat16 [384, 256], P('col'), may hold values from -0.3125 to 0.3125
- gain_first: float32 [128], replicated, may hold values from 0.1 to 1.9
- first_in: bfloat16 [128, 1024], replicated, may hold values from -0.5 to 0.5
- first_out: bfloat16 [512, 128], replicated, may hold values from -0.25 to 0.25
- gain_second: float32 [128], replicated, may hold values from 0.1 to 1.9
- second_in: bfloat16 [128, 1024], replicated, may hold values from -0.5 to 0.5
- second_out: bfloat16 [512, 128], replicated, may hold values from -0.25 to 0.25
- head_weight: bfloat16 [128, 64], replicated, may hold values from -1.5 to 1.5
- pae_bins: int32 [512, 512], P('row', 'col'), may hold values from 0 to 63
- chain_perm: int32 [512], replicated, may hold values from 0 to 511, as said below
- resolved_counts: int32 [4, 8], P('row'), may hold values from 1 to 256, 1024 in all within a row
- tile_order: int32 [4, 2048], P('row', 'col'), may hold values from 0 to 255, as said below
Outputs:
- pair_grad: bfloat16 [512, 512, 128], P('row', 'col')
- single_grad: float32 [512, 384], P('row', 'col')
- second_in_grad: float32 [128, 1024], replicated
- second_out_grad: float32 [512, 128], replicated
- head_grad: float32 [128, 64], replicated
Inputs may be any that keep to these rules, and one draw needn't show every extreme that they name: chain_perm maps every aligned group of 64 tokens onto itself, moving whole aligned runs of 16 tokens and keeping the order inside a run. Each row of resolved_counts sums to 1024, and its largest entry is 256. In each row of tile_order, entries b * 256 to (b + 1) * 256 - 1 are a permutation of 0 to 255.
All inputs are finite; a program needn't handle non-finite values.
Results may differ from a plain program's by a relative error of at most 0.011.
Values may be sent and summed in bfloat16 or wider, within the bound.
No kernel may reach another device: no remote copies, remote signals or barrier semaphores. Data moves between devices by JAX's collectives and lax.ppermute only.
A program may use at most 64 MiB of HBM per device.

v0:
```python
import jax
import jax.numpy as jnp
from jax import lax
from jax.sharding import PartitionSpec as P

TILE = 32


def contract(left_op, right_op, left_dim, right_dim):
    return lax.dot_general(
        left_op,
        right_op,
        (((left_dim,), (right_dim,)), ((), ())),
        preferred_element_type=jnp.float32,
    )


def block_size(extent, per_item, limit):
    best = 1
    for candidate in range(1, extent + 1):
        if extent % candidate == 0 and candidate * per_item <= limit:
            best = candidate
    return best


def transition_forward(start_z, gain_vec, w_in, w_out):
    hidden_units = w_out.shape[0]
    average = jnp.mean(start_z, axis=-1, keepdims=True)
    centred = start_z - average
    scaling = lax.rsqrt(jnp.mean(centred * centred, axis=-1, keepdims=True) + 1e-05)
    normed = centred * scaling
    inputs = (normed * gain_vec).astype(jnp.bfloat16)
    gate_up = jnp.dot(inputs, w_in, preferred_element_type=jnp.float32)
    gate_part = gate_up[:, :hidden_units]
    up_part = gate_up[:, hidden_units:]
    gate_sig = jax.nn.sigmoid(gate_part)
    hidden_act = (gate_part * gate_sig * up_part).astype(jnp.bfloat16)
    result = jnp.dot(hidden_act, w_out, preferred_element_type=jnp.float32)
    return (result, (normed, scaling, inputs, gate_part, up_part, gate_sig, hidden_act))


def transition_backward(saved, grad_out, gain_vec, w_in, w_out, with_weights):
    normed, scaling, inputs, gate_part, up_part, gate_sig, hidden_act = saved
    grad_hidden = contract(grad_out, w_out, 1, 1)
    grad_gate = grad_hidden * up_part * gate_sig * (1.0 + gate_part * (1.0 - gate_sig))
    grad_up = grad_hidden * gate_part * gate_sig
    grad_both = jnp.concatenate([grad_gate, grad_up], axis=1).astype(jnp.bfloat16)
    grad_normed = contract(grad_both, w_in, 1, 1) * gain_vec
    grad_field = scaling * (
        grad_normed
        - jnp.mean(grad_normed, axis=-1, keepdims=True)
        - normed * jnp.mean(grad_normed * normed, axis=-1, keepdims=True)
    )
    if with_weights:
        return (grad_field, contract(inputs, grad_both, 0, 0), contract(hidden_act, grad_out, 0, 0))
    return (grad_field, None, None)


def head_step(rounded_z, targets, keep_mask, head_weight):
    logits = jnp.dot(rounded_z, head_weight, preferred_element_type=jnp.float32)
    exponent = jnp.exp(logits - jnp.max(logits, axis=-1, keepdims=True))
    probability = exponent / jnp.sum(exponent, axis=-1, keepdims=True)
    onehot = (targets[:, None] == lax.broadcasted_iota(jnp.int32, logits.shape, 1)).astype(
        jnp.float32
    )
    grad_logits = ((probability - onehot) * keep_mask[:, None]).astype(jnp.bfloat16)
    return (
        contract(grad_logits, head_weight, 1, 1).astype(jnp.bfloat16),
        contract(rounded_z, grad_logits, 0, 0),
    )


def second_step(pair_one, targets, live_mask, gain_second, second_in, second_out, head_weight):
    start_f = pair_one.astype(jnp.float32)
    delta, saved = transition_forward(start_f, gain_second, second_in, second_out)
    rounded_z = (start_f + live_mask[:, None] * delta).astype(jnp.bfloat16)
    grad_two, head_part = head_step(rounded_z, targets, jnp.ones_like(live_mask), head_weight)
    masked_out = jnp.where(live_mask[:, None] > 0, grad_two, jnp.zeros((), jnp.bfloat16))
    back_field, in_part, out_part = transition_backward(
        saved, masked_out, gain_second, second_in, second_out, True
    )
    return (
        (grad_two.astype(jnp.float32) + back_field).astype(jnp.bfloat16),
        in_part,
        out_part,
        head_part,
    )


def local(
    singles,
    pair_in,
    proj_weight,
    gain_first,
    first_in,
    first_out,
    gain_second,
    second_in,
    second_out,
    head_weight,
    pae_bins,
    chain_perm,
    resolved_counts,
    tile_order,
):
    rows_dev, cols_dev, width = pair_in.shape
    tile_len = TILE
    tiles_dev = rows_dev * cols_dev // tile_len
    token_count = chain_perm.shape[0]
    row_index = lax.axis_index("row")
    col_index = lax.axis_index("col")
    partial_proj = jnp.dot(singles, proj_weight, preferred_element_type=jnp.float32)
    projected = lax.psum(partial_proj, "col")
    left_part = projected[:, :width]
    right_part = projected[:, width:].astype(jnp.bfloat16)
    col_start = col_index * cols_dev
    right_all = lax.all_gather(right_part, "row", axis=0, tiled=True)
    col_right = lax.dynamic_slice_in_dim(right_all, col_start, cols_dev, 0)
    col_right_f = col_right.astype(jnp.float32)
    block_rows = block_size(rows_dev, cols_dev, 1024)
    row_blocks = rows_dev // block_rows
    block_pairs = block_rows * cols_dev

    def start_field(block_index):
        first_row = block_index * block_rows
        pair_rows = lax.dynamic_slice_in_dim(pair_in, first_row, block_rows, 0).astype(jnp.float32)
        left_rows = lax.dynamic_slice_in_dim(left_part, first_row, block_rows, 0)
        field_rows = pair_rows + left_rows[:, None, :] + col_right_f[None, :, :]
        return field_rows.reshape(block_pairs, width)

    def forward_block(block_index):
        start_z = start_field(block_index)
        delta, unused_saved = transition_forward(start_z, gain_first, first_in, first_out)
        return (start_z + delta).astype(jnp.bfloat16)

    block_ids = jnp.arange(row_blocks, dtype=jnp.int32)
    pair_one = lax.map(forward_block, block_ids).reshape(rows_dev * cols_dev, width)
    live_count = resolved_counts[0, col_index]
    order_list = tile_order[0]
    tile_iota = jnp.arange(tiles_dev, dtype=jnp.int32)
    rank_of = jnp.sum(
        jnp.where(order_list[None, :] == tile_iota[:, None], tile_iota[None, :], 0), axis=1
    )
    tile_live = rank_of < live_count
    pair_live = jnp.repeat(tile_live, tile_len).astype(jnp.float32)
    perm_rows = (
        lax.dynamic_slice_in_dim(chain_perm, row_index * rows_dev, rows_dev, 0)
        - row_index * rows_dev
    )
    perm_cols = lax.dynamic_slice_in_dim(chain_perm, col_start, cols_dev, 0) - col_start
    targets = jnp.take(jnp.take(pae_bins, perm_rows, axis=0), perm_cols, axis=1).reshape(
        rows_dev * cols_dev
    )
    pair_stack = pair_one.reshape(row_blocks, block_pairs, width)
    target_stack = targets.reshape(row_blocks, block_pairs)
    live_stack = pair_live.reshape(row_blocks, block_pairs)
    zero_in = jnp.zeros(second_in.shape, jnp.float32)
    zero_out = jnp.zeros(second_out.shape, jnp.float32)
    zero_head = jnp.zeros(head_weight.shape, jnp.float32)

    def local_block(running, operands):
        grad_one, in_part, out_part, head_part = second_step(
            operands[0], operands[1], operands[2], gain_second, second_in, second_out, head_weight
        )
        return ((running[0] + in_part, running[1] + out_part, running[2] + head_part), grad_one)

    weight_sums, grad_stack = lax.scan(
        local_block, (zero_in, zero_out, zero_head), (pair_stack, target_stack, live_stack)
    )
    grad_one_all = grad_stack.reshape(rows_dev * cols_dev, width)
    grad_one_stack = grad_one_all.reshape(row_blocks, block_pairs, width)

    def backward_block(running, operands):
        block_index, grad_one = operands
        start_z = start_field(block_index)
        unused_delta, saved = transition_forward(start_z, gain_first, first_in, first_out)
        back_field, unused_in, unused_out = transition_backward(
            saved, grad_one, gain_first, first_in, first_out, False
        )
        grad_zero = (grad_one.astype(jnp.float32) + back_field).reshape(block_rows, cols_dev, width)
        return (
            running + jnp.sum(grad_zero, axis=0),
            (grad_zero.astype(jnp.bfloat16), jnp.sum(grad_zero, axis=1)),
        )

    right_grad, (pair_grad_stack, left_stack) = lax.scan(
        backward_block, jnp.zeros((cols_dev, width), jnp.float32), (block_ids, grad_one_stack)
    )
    pair_grad = pair_grad_stack.reshape(rows_dev, cols_dev, width)
    left_grad = left_stack.reshape(rows_dev, width)
    token_part = jnp.zeros((token_count, 2 * width), jnp.float32)
    token_part = lax.dynamic_update_slice(token_part, left_grad, (row_index * rows_dev, 0))
    token_part = lax.dynamic_update_slice(token_part, right_grad, (col_start, width))
    token_total, in_total, out_total, head_total = lax.psum(
        (token_part, weight_sums[0], weight_sums[1], weight_sums[2]), ("row", "col")
    )
    token_rows = lax.dynamic_slice_in_dim(token_total, row_index * rows_dev, rows_dev, 0).astype(
        jnp.bfloat16
    )
    single_grad = contract(token_rows, proj_weight, 1, 1)
    return (
        pair_grad,
        single_grad,
        in_total / token_count,
        out_total / token_count,
        head_total / token_count,
    )


def solution(mesh):
    in_specs = (
        P("row", "col"),
        P("row", "col", None),
        P("col", None),
        P(),
        P(),
        P(),
        P(),
        P(),
        P(),
        P(),
        P("row", "col"),
        P(),
        P("row", None),
        P("row", "col"),
    )
    out_specs = (P("row", "col", None), P("row", "col"), P(), P(), P())
    return jax.shard_map(local, mesh=mesh, in_specs=in_specs, out_specs=out_specs, check_vma=False)
```

profile of v0, /device:TPU:0, one launch (start us, length us, event | category | flops | bytes accessed | tf_op | source)
XLA Modules:
  0.0 514.7 jit_solution(13817888592120725442)
XLA Ops:
  17.3 49.4 %all-reduce.6.cloned.1.call-done = f32[128,256]{1,0:T(8,128)} async-done(((f32[128,256]{1,0:T(8,128)}), f32[128,256]{1,0:T(8,128)}) %all-reduce.6.cloned.1.call-update) | async-done | bytes 131088 | tf_op jit(solution)/shard_map/psum | solution.py:113
  67.6 13.4 %all_gather.3 = bf16[512,128]{1,0:T(8,128)(2,1)S(1)} all-gather(bf16[128,128]{1,0:T(8,128)(2,1)S(1)} %slice.64), channel_id=1, replica_groups=mesh['row'=4,'col'=8] {'row'}, dimensions={0}, use_global_device_ids=true | all-gather | bytes 163840 | tf_op jit(solution)/shard_map/all_gather | solution.py:117
  81.3 45.5 %while.42 = (s32[]{:T(128)}, bf16[8,1024,128]{2,1,0:T(8,128)(2,1)S(1)}, s32[8]{0:T(128)S(1)}, bf16[128,64,128]{2,1,0:T(8,128)(2,1)}, f32[128,128]{1,0:T(8,128)S(...) while((s32[]{:T(128)}, ...), condition=%wide.region_4.5_spmd, body=%wide.region_1.4_spmd.sunk | while | flops 407897088 | bytes 11817671 | solution.py:137
  128.5 146.6 %while.43 = (s32[]{:T(128)}, f32[128,1024]{1,0:T(8,128)}, f32[512,128]{1,0:T(8,128)}, f32[128,64]{0,1:T(8,128)}, bf16[8,1024,128]{2,1,0:T(8,128)(2,1)}, /*index=...) while((s32[]{:T(128)}, f32[128,1024]{1,0:T(8,128)}, ...), condition=%wide.region_13.14_spmd.clone, body=%wide.region_6.13_spmd.clone.sunk | while | flops 1283276800 | bytes 52164016 | solution.py:167
  135.7 2.5 fusion.147
  139.6 2.0 convolution_add_fusion.6
  141.6 2.2 convolution_add_fusion.5
  143.8 2.0 fusion.146
  153.0 2.5 fusion.147
  156.9 2.0 convolution_add_fusion.6
  158.9 2.3 convolution_add_fusion.5
  161.2 3.1 fusion.146
  171.5 2.5 fusion.147
  175.3 2.0 convolution_add_fusion.6
  177.3 2.3 convolution_add_fusion.5
  179.6 3.1 fusion.146
  189.9 2.5 fusion.147
  193.8 2.0 convolution_add_fusion.6
  195.8 2.3 convolution_add_fusion.5
  198.1 3.1 fusion.146
  208.4 2.5 fusion.147
  212.3 2.0 convolution_add_fusion.6
  214.3 2.3 convolution_add_fusion.5
  216.6 3.1 fusion.146
  226.9 2.5 fusion.147
  230.8 2.0 convolution_add_fusion.6
  232.7 2.3 convolution_add_fusion.5
  235.0 3.1 fusion.146
  245.3 2.5 fusion.147
  249.2 2.0 convolution_add_fusion.6
  251.2 2.3 convolution_add_fusion.5
  253.5 3.1 fusion.146
  263.8 2.5 fusion.147
  267.7 2.0 convolution_add_fusion.6
  269.7 2.3 convolution_add_fusion.5
  272.0 3.1 fusion.146
  275.1 99.2 %while.44 = (s32[]{:T(128)}, f32[64,128]{1,0:T(8,128)S(1)}, bf16[8,16,64,128]{3,2,1,0:T(8,128)(2,1)}, f32[8,16,128]{2,1,0:T(8,128)}, bf16[8,1024,128]{2,1,0:T(8,...) while((s32[]{:T(128)}, f32[64,128]{1,0:T(8,128)S(1)}, ...), condition=%wide.region_21.22_spmd.clone, body=%wide.region_14.21_spmd.clone.sunk | while | flops 686169088 | bytes 21199632 | solution.py:186
  281.1 2.1 fusion.155
  293.5 2.1 fusion.155
  305.9 2.1 fusion.155
  318.3 2.1 fusion.155
  330.6 2.1 fusion.155
  343.0 2.1 fusion.155
  355.4 2.1 fusion.155
  367.8 2.1 fusion.155
  375.2 47.0 %all-reduce.9 = (bf16[512,256]{1,0:T(8,128)(2,1)S(1)}, f32[128,64]{0,1:T(8,128)S(1)}) all-reduce(f32[512,256]{1,0:T(8,128)S(1)} %constant_dynamic-update-slice_fusion.2, f32[128,64]{0,1:T(8,128)S(1)} %copy-done.11), channel_id=1, replica_groups=mesh['row'=4,'col'=8] {'row','col'}, use_global_device_ids=true, to_apply=%region_22.23 | all-reduce | flops 139264 | bytes 851968 | tf_op jit(solution)/shard_map/psum | solution.py:194
  423.6 80.7 %all-reduce.8.cloned.1.call-done = (f32[128,1024]{1,0:T(8,128)}, f32[512,128]{1,0:T(8,128)}) async-done(((f32[128,1024]{1,0:T(8,128)}, f32[512,128]{1,0:T(8,128)}), (f32[128,1024]{1,0:T(8,128)}, f32[512,128]{1,0:T(8,128)})) %all-reduce.8.cloned.1.call-update) | async-done | bytes 786448 | tf_op jit(solution)/shard_map/psum | solution.py:194
  504.3 1.9 broadcast_multiply_fusion.7
  (585 shorter events, 201.2 us)
Async XLA Ops:
  7.2 7.9 %copy-start.15 = (s32[1,8]{1,0:T(1,128)S(1)}, s32[1,8]{1,0:T(1,128)}, u32[]{:S(2)}) copy-start(s32[1,8]{1,0:T(1,128)} %param.32) | copy-start | bytes 100
  7.2 59.5 %all-reduce.6.cloned.1.call-start = ((), (), s32[]{:S(2)}) async-start(), calls=%async_computation | async-start | bytes 262144 | tf_op jit(solution)/shard_map/psum | solution.py:113
  9.5 494.8 %all-reduce.8.cloned.1.call-start = ((), (), s32[]{:S(2)}) async-start(), calls=%async_computation.1 | async-start | bytes 1572864 | tf_op jit(solution)/shard_map/psum | solution.py:194
  11.8 69.5 %copy-start.1 = (bf16[128,1024]{1,0:T(8,128)(2,1)S(1)}, bf16[128,1024]{1,0:T(8,128)(2,1)}, u32[]{:S(2)}) copy-start(bf16[128,1024]{1,0:T(8,128)(2,1)} %param.24) | copy-start | bytes 786436
  11.8 69.5 %copy-start.10 = (f32[128]{0:T(128)S(1)}, f32[128]{0:T(128)}, u32[]{:S(2)}) copy-start(f32[128]{0:T(128)} %param.23) | copy-start | bytes 1540
  11.8 69.5 %copy-start.13 = (bf16[512,128]{1,0:T(8,128)(2,1)S(1)}, bf16[512,128]{1,0:T(8,128)(2,1)}, u32[]{:S(2)}) copy-start(bf16[512,128]{1,0:T(8,128)(2,1)} %param.25) | copy-start | bytes 393220
  66.7 14.6 %slice-start = ((f32[128,256]{1,0:T(8,128)}), f32[128,128]{1,0:T(8,128)S(1)}, s32[]{:S(2)}) async-start(f32[128,256]{1,0:T(8,128)} %all-reduce.6.cloned.1.call-done), calls=%async_computation.2 | async-start | bytes 131072 | tf_op jit(solution)/shard_map/slice | solution.py:114
  134.0 4.3 copy-start.4
  135.7 2.5 copy-start.16
  135.7 2.5 copy-start.18
  139.6 4.2 copy-start.17
  139.6 4.2 copy-start.19
  151.2 4.3 copy-start.4
  153.0 2.5 copy-start.16
  153.0 2.5 copy-start.18
  156.9 4.3 copy-start.17
  156.9 4.3 copy-start.19
  161.2 3.1 copy-start.6
  169.7 4.3 copy-start.4
  171.4 2.5 copy-start.16
  175.3 4.3 copy-start.17
  175.3 4.3 copy-start.19
  179.6 3.1 copy-start.6
  188.2 4.3 copy-start.4
  193.8 4.3 copy-start.17
  193.8 4.3 copy-start.19
  198.1 3.1 copy-start.6
  206.6 4.3 copy-start.4
  212.3 4.3 copy-start.17
  212.3 4.3 copy-start.19
  216.6 3.1 copy-start.6
  225.1 4.3 copy-start.4
  226.9 2.5 copy-start.16
  226.9 2.5 copy-start.18
  230.7 4.3 copy-start.17
  230.8 4.3 copy-start.19
  235.0 3.1 copy-start.6
  243.6 4.3 copy-start.4
  249.2 4.3 copy-start.17
  249.2 4.3 copy-start.19
  253.5 3.1 copy-start.6
  262.0 4.3 copy-start.4
  263.8 2.5 copy-start.16
  263.8 2.5 copy-start.18
  267.7 4.3 copy-start.17
  267.7 4.3 copy-start.19
  272.0 3.1 copy-start.6
  275.1 100.1 %copy-start.11 = (f32[128,64]{0,1:T(8,128)S(1)}, f32[128,64]{0,1:T(8,128)}, u32[]{:S(2)}) copy-start(f32[128,64]{0,1:T(8,128)} %get-tuple-element.753) | copy-start | bytes 98308
  (45 other events, 58.1 us)
Sparse Core Ops, SparseCore 0:
  11.1 55.6 all-reduce.5
  375.3 128.9 all-reduce.7
where the time goes:
time: 519 us; the launch traced here: 515 us
  matrix products  154 us (30%)
  waiting for transfers between devices  130 us (25%)
  other arithmetic  87.4 us (17%)
  blocking collectives  60.4 us (12%)
  local copies, waits for them, and re-layouts  55.6 us (11%)
  between operations  14.3 us (3%)
  loops' own time  12.4 us (2%)
    dot_general x65, matrix products, contract(): lax.dot_general(left_op, right_op, (((left_dim,), (right_dim,)), ((), ())...  122 us
    psum x1, waiting for transfers between devices, local(): lax.psum((token_part, weight_sums[0], weight_sums[1], weight_sums[2]), ('...  80.7 us
    psum x1, waiting for transfers between devices, local(): projected = lax.psum(partial_proj, 'col')  49.4 us
    psum x1, blocking collectives, local(): lax.psum((token_part, weight_sums[0], weight_sums[1], weight_sums[2]), ('...  47 us
    reduce_sum x24, other arithmetic, transition_forward(): jnp.mean(centred * centred, axis=-1, keepdims=True) + 1e-05  24.6 us
    reduce_sum x24, other arithmetic, transition_forward(): average = jnp.mean(start_z, axis=-1, keepdims=True)  19.7 us
    dot_general x24, matrix products, transition_forward(): gate_up = jnp.dot(inputs, w_in, preferred_element_type=jnp.float32)  18.7 us
    all_gather x1, blocking collectives, local(): right_all = lax.all_gather(right_part, 'row', axis=0, tiled=True)  13.4 us
  transfers between devices with their start and end apart: 2, of which 2 were waited for; matrix products, arithmetic and copies ran while one was open for 2% of the time, Pallas kernels for 0%

commit v1 on v0

v1 whole, which is shorter than its diff:
```python
import functools

import jax
import jax.numpy as jnp
from jax import lax
from jax.experimental import pallas as pl
from jax.experimental.pallas import tpu as pltpu
from jax.sharding import PartitionSpec as P

TILE = 32
BLOCK_ROWS = 32
CHUNK = 256
F32 = jnp.float32
BF16 = jnp.bfloat16


def dot(left_op, right_op, left_dim=1, right_dim=0):
    return lax.dot_general(
        left_op,
        right_op,
        (((left_dim,), (right_dim,)), ((), ())),
        preferred_element_type=F32,
    )


def norm(field):
    centred = field - jnp.mean(field, axis=-1, keepdims=True)
    scaling = lax.rsqrt(jnp.mean(centred * centred, axis=-1, keepdims=True) + 1e-05)
    return centred * scaling, scaling


def forward(inputs, w_in, w_out, act_ref, slope_ref, hidden_ref):
    hid = w_out.shape[0]
    result = None
    for j in range(0, hid, CHUNK):
        half_gate = dot(inputs, w_in[:, j : j + CHUNK])
        up = dot(inputs, w_in[:, hid + j : hid + j + CHUNK])
        twice_sig = 1.0 + jnp.tanh(half_gate)
        act = half_gate * twice_sig
        hidden = (act * up).astype(BF16)
        act_ref[:, j : j + CHUNK] = act
        slope_ref[:, j : j + CHUNK] = up * (twice_sig + act * (2.0 - twice_sig))
        if hidden_ref is not None:
            hidden_ref[:, j : j + CHUNK] = hidden
        part = dot(hidden, w_out[j : j + CHUNK, :])
        result = part if result is None else result + part
    return result


def backward(grad_out, normed, scaling, gain, w_in, w_out, act_ref, slope_ref, both_ref):
    hid = w_out.shape[0]
    grad_normed = None
    for j in range(0, hid, CHUNK):
        grad_hidden = dot(grad_out, w_out[j : j + CHUNK, :], 1, 1)
        grad_gate = (grad_hidden * slope_ref[:, j : j + CHUNK]).astype(BF16)
        grad_up = (grad_hidden * act_ref[:, j : j + CHUNK]).astype(BF16)
        if both_ref is not None:
            both_ref[:, j : j + CHUNK] = grad_gate
            both_ref[:, hid + j : hid + j + CHUNK] = grad_up
        part = dot(grad_gate, w_in[:, j : j + CHUNK], 1, 1)
        part = part + dot(grad_up, w_in[:, hid + j : hid + j + CHUNK], 1, 1)
        grad_normed = part if grad_normed is None else grad_normed + part
    grad_normed = grad_normed * gain
    mean = jnp.mean(grad_normed, axis=-1, keepdims=True)
    slant = jnp.mean(grad_normed * normed, axis=-1, keepdims=True)
    return scaling * (grad_normed - mean - normed * slant)


def pair_kernel(
    tokens,
    counts_ref,
    order_ref,
    pair_ref,
    left_ref,
    right_ref,
    bins_ref,
    perm_rows_ref,
    perm_cols_ref,
    gain_first_ref,
    first_in_ref,
    first_out_ref,
    gain_second_ref,
    second_in_ref,
    second_out_ref,
    head_ref,
    pair_grad_ref,
    left_grad_ref,
    right_grad_ref,
    weights_ref,
    live_ref,
    target_ref,
    first_half,
    second_half,
    act_one,
    slope_one,
    act_two,
    slope_two,
    hidden_two,
    both_two,
    in_sum,
    out_sum,
    head_sum,
):
    block_rows, cols, width = pair_ref.shape
    pairs = block_rows * cols
    hid = first_out_ref.shape[0]
    tiles = pairs // TILE
    step = pl.program_id(0)
    blocks = target_ref.shape[0]

    @pl.when(step == 0)
    def _():
        right_grad_ref[...] = jnp.zeros_like(right_grad_ref)
        in_sum[...] = jnp.zeros_like(in_sum)
        out_sum[...] = jnp.zeros_like(out_sum)
        head_sum[...] = jnp.zeros_like(head_sum)
        for half, whole in ((first_half, first_in_ref), (second_half, second_in_ref)):
            half[:, :hid] = whole[:, :hid] * jnp.asarray(0.5, BF16)
            half[:, hid:] = whole[:, hid:]
        count = counts_ref[0, lax.axis_index("col")]

        def place(t, carry):
            live_ref[order_ref[0, t]] = jnp.where(t < count, 1.0, 0.0).astype(F32)
            return carry

        lax.fori_loop(0, order_ref.shape[1], place, 0, unroll=8)
        rows = bins_ref.shape[0]
        row_index, col_index = lax.axis_index("row"), lax.axis_index("col")
        perm_rows = perm_rows_ref[pl.ds(row_index, 1), :] - row_index * rows
        perm_cols = perm_cols_ref[pl.ds(col_index, 1), :] - col_index * cols
        pick_rows = (lax.broadcasted_iota(jnp.int32, (rows, rows), 0) == perm_rows).astype(BF16)
        pick_cols = (lax.broadcasted_iota(jnp.int32, (cols, cols), 0) == perm_cols).astype(BF16)
        bins = bins_ref[...].astype(F32).astype(BF16)
        moved = dot(bins, pick_rows, 0, 0).astype(BF16)
        moved = dot(pick_cols, moved, 0, 0)
        for b in range(blocks):
            target_ref[b] = moved[:, b * block_rows : (b + 1) * block_rows].astype(jnp.int32)

    field = pair_ref[...].astype(F32) + left_ref[...][:, None, :]
    field = (field + right_ref[...].astype(F32)[None]).reshape(pairs, width)
    normed_one, scaling_one = norm(field)
    inputs_one = (normed_one * gain_first_ref[...]).astype(BF16)
    delta_one = forward(inputs_one, first_half, first_out_ref, act_one, slope_one, None)
    pair_one = (field + delta_one).astype(BF16).astype(F32)

    normed_two, scaling_two = norm(pair_one)
    inputs_two = (normed_two * gain_second_ref[...]).astype(BF16)
    delta_two = forward(inputs_two, second_half, second_out_ref, act_two, slope_two, hidden_two)
    live = [live_ref[step * tiles + t] for t in range(tiles)]

    def masked(x):
        return jnp.concatenate(
            [x[t * TILE : (t + 1) * TILE] * live[t] for t in range(tiles)], axis=0
        )

    pair_two = (pair_one + masked(delta_two)).astype(BF16)

    logits = dot(pair_two, head_ref[...])
    exponent = jnp.exp(logits - jnp.max(logits, axis=-1, keepdims=True))
    probability = exponent * (1.0 / jnp.sum(exponent, axis=-1, keepdims=True))
    target = target_ref[step]
    bin_ids = lax.broadcasted_iota(jnp.int32, (cols, logits.shape[-1]), 1)
    onehot = jnp.concatenate(
        [(target[:, r : r + 1] == bin_ids).astype(F32) for r in range(block_rows)], axis=0
    )
    grad_logits = (probability - onehot).astype(BF16)
    grad_two = dot(grad_logits, head_ref[...], 1, 1).astype(BF16).astype(F32)
    head_sum[...] += dot(pair_two, grad_logits, 0, 0)

    grad_delta = masked(grad_two).astype(BF16)
    back_two = backward(
        grad_delta,
        normed_two,
        scaling_two,
        gain_second_ref[...],
        second_half,
        second_out_ref,
        act_two,
        slope_two,
        both_two,
    )
    in_sum[...] += dot(inputs_two, both_two[...], 0, 0)
    out_sum[...] += dot(grad_delta, hidden_two[...], 0, 0)

    grad_one = (grad_two + back_two).astype(BF16)
    back_one = backward(
        grad_one,
        normed_one,
        scaling_one,
        gain_first_ref[...],
        first_half,
        first_out_ref,
        act_one,
        slope_one,
        None,
    )
    grad_zero = (grad_one.astype(F32) + back_one).reshape(block_rows, cols, width)
    pair_grad_ref[...] = grad_zero.astype(BF16)
    left_grad_ref[...] = jnp.sum(grad_zero, axis=1)
    right_grad_ref[...] += jnp.sum(grad_zero, axis=0)

    @pl.when(step == pl.num_programs(0) - 1)
    def _():
        scale = 1.0 / tokens
        row = 0
        for j in range(0, 2 * hid, width):
            factor = scale * 0.5 if j < hid else scale
            weights_ref[row : row + width, :] = (in_sum[:, j : j + width] * factor).astype(BF16)
            row += width
        for j in range(0, hid, width):
            part = jnp.transpose(out_sum[:, j : j + width])
            weights_ref[row : row + width, :] = (part * scale).astype(BF16)
            row += width
        half = width // 2
        packed = jnp.concatenate([head_sum[:half, :], head_sum[half:, :]], axis=1) * scale
        weights_ref[row : row + half, :] = packed.astype(BF16)
        row += half
        if row < weights_ref.shape[0]:
            rest = (weights_ref.shape[0] - row, width)
            weights_ref[row:, :] = jnp.zeros(rest, BF16)


def pair_grid(
    counts,
    order,
    pair_in,
    left_part,
    right_part,
    pae_bins,
    perm_rows,
    perm_cols,
    gain_first,
    first_in,
    first_out,
    gain_second,
    second_in,
    second_out,
    head_weight,
    tokens,
    weight_rows,
):
    rows, cols, width = pair_in.shape
    block_rows = min(BLOCK_ROWS, rows)
    pairs = block_rows * cols
    hid = first_out.shape[0]
    bins = head_weight.shape[1]

    def whole(x):
        return pl.BlockSpec(x.shape, lambda i, *_: (0,) * x.ndim)

    def fixed(*shape):
        return pl.BlockSpec(shape, lambda i, *_: (0,) * len(shape))

    small = (
        right_part,
        pae_bins,
        perm_rows,
        perm_cols,
        gain_first,
        first_in,
        first_out,
        gain_second,
        second_in,
        second_out,
        head_weight,
    )
    grid_spec = pltpu.PrefetchScalarGridSpec(
        num_scalar_prefetch=2,
        grid=(rows // block_rows,),
        in_specs=[
            pl.BlockSpec((block_rows, cols, width), lambda i, *_: (i, 0, 0)),
            pl.BlockSpec((block_rows, width), lambda i, *_: (i, 0)),
        ]
        + [whole(x) for x in small],
        out_specs=[
            pl.BlockSpec((block_rows, cols, width), lambda i, *_: (i, 0, 0)),
            pl.BlockSpec((block_rows, width), lambda i, *_: (i, 0)),
            fixed(cols, width),
            fixed(weight_rows, width),
        ],
        scratch_shapes=[
            pltpu.SMEM((rows * cols // TILE,), F32),
            pltpu.VMEM((rows // block_rows, cols, block_rows), jnp.int32),
            pltpu.VMEM((width, 2 * hid), BF16),
            pltpu.VMEM((width, 2 * hid), BF16),
            pltpu.VMEM((pairs, hid), F32),
            pltpu.VMEM((pairs, hid), F32),
            pltpu.VMEM((pairs, hid), F32),
            pltpu.VMEM((pairs, hid), F32),
            pltpu.VMEM((pairs, hid), BF16),
            pltpu.VMEM((pairs, 2 * hid), BF16),
            pltpu.VMEM((width, 2 * hid), F32),
            pltpu.VMEM((width, hid), F32),
            pltpu.VMEM((width, bins), F32),
        ],
    )
    macs = rows * cols * width * (16 * hid + 3 * bins)
    return pl.pallas_call(
        functools.partial(pair_kernel, tokens),
        grid_spec=grid_spec,
        out_shape=[
            jax.ShapeDtypeStruct((rows, cols, width), BF16),
            jax.ShapeDtypeStruct((rows, width), F32),
            jax.ShapeDtypeStruct((cols, width), F32),
            jax.ShapeDtypeStruct((weight_rows, width), BF16),
        ],
        compiler_params=pltpu.CompilerParams(
            vmem_limit_bytes=56 << 20, dimension_semantics=("arbitrary",)
        ),
        cost_estimate=pl.CostEstimate(
            flops=2 * macs,
            bytes_accessed=4 * rows * cols * width,
            transcendentals=2 * rows * cols * hid,
        ),
    )(counts, order, pair_in, left_part, *small)


def swap(x, axis, size, mask):
    return lax.ppermute(x, axis, [(i, i ^ mask) for i in range(size)])


def tree_sum(parts):
    parts = [p.astype(F32) for p in parts]
    while len(parts) > 1:
        parts = [parts[k] + parts[k + 1] for k in range(0, len(parts), 2)]
    return parts[0]


def in_order(parts, index):
    parts = list(parts)
    bit = 1
    while bit < len(parts):
        parts = [
            jnp.where((index & bit) != 0, parts[k ^ bit], parts[k]) for k in range(len(parts))
        ]
        bit *= 2
    return jnp.stack(parts)


def local(
    n_row,
    n_col,
    singles,
    pair_in,
    proj_weight,
    gain_first,
    first_in,
    first_out,
    gain_second,
    second_in,
    second_out,
    head_weight,
    pae_bins,
    chain_perm,
    resolved_counts,
    tile_order,
):
    rows, cols, width = pair_in.shape
    tokens = chain_perm.shape[0]
    hid = first_out.shape[0]
    bins = head_weight.shape[1]
    row_index = lax.axis_index("row")
    col_index = lax.axis_index("col")
    ratio = rows // cols

    joined = jnp.concatenate([singles.T, proj_weight], axis=1)
    joined = lax.all_gather(joined, "col", axis=0, tiled=True)
    projected = dot(joined[:, :rows], joined[:, rows:], 0, 0)
    left_part = projected[:, :width]
    own_half = lax.dynamic_slice_in_dim(
        projected[:, width:], (col_index % ratio) * cols, cols, 0
    ).astype(BF16)
    right_part = lax.ppermute(
        own_half,
        ("row", "col"),
        [
            ((c // ratio) * n_col + z * ratio + c % ratio, z * n_col + c)
            for z in range(n_row)
            for c in range(n_col)
        ],
    )

    used_rows = 3 * hid + width // 2
    share = -(-used_rows // (n_col * 16)) * 16
    pair_grad, left_grad, right_grad, weights = pair_grid(
        resolved_counts,
        tile_order,
        pair_in,
        left_part,
        right_part,
        pae_bins,
        chain_perm.reshape(n_row, rows),
        chain_perm.reshape(n_col, cols),
        gain_first.reshape(1, width),
        first_in,
        first_out,
        gain_second.reshape(1, width),
        second_in,
        second_out,
        head_weight,
        tokens,
        share * n_col,
    )

    right_sent = right_grad.astype(BF16)
    right_parts = [right_sent] + [swap(right_sent, "row", n_row, k) for k in range(1, n_row)]
    right_total = tree_sum(right_parts).astype(BF16)
    spread = [
        lax.ppermute(
            right_total,
            ("row", "col"),
            [
                (z * n_col + c, (c // ratio) * n_col + z * ratio + (p ^ (c % ratio)))
                for z in range(n_row)
                for c in range(n_col)
            ],
        )
        for p in range(ratio)
    ]
    right_tokens = in_order(spread, col_index % ratio).reshape(rows, width)

    left_share = left_grad.astype(BF16).reshape(n_col, rows // n_col, width)
    buffer = jnp.concatenate([weights.reshape(n_col, share, width), left_share], axis=1)
    depth = buffer.shape[1]
    chips = n_col // 2
    chip, core = col_index // 2, col_index % 2
    buffer = buffer.reshape(chips, 2, depth, width)
    kept = lax.dynamic_index_in_dim(buffer, core, 1, keepdims=False)
    sent = lax.dynamic_index_in_dim(buffer, 1 - core, 1, keepdims=False)
    buffer = tree_sum([kept, swap(sent, "col", n_col, 1)]).astype(BF16)
    parts = [lax.dynamic_index_in_dim(buffer, chip, 0, keepdims=False)]
    for k in range(1, chips):
        sent = lax.dynamic_index_in_dim(buffer, chip ^ k, 0, keepdims=False)
        parts.append(swap(sent, "col", n_col, 2 * k))
    buffer = tree_sum(parts).astype(BF16)
    own = buffer[:share]
    own = tree_sum([own] + [swap(own, "row", n_row, k) for k in range(1, n_row)]).astype(BF16)
    buffer = jnp.concatenate([own, buffer[share:]], axis=0)
    buffer = in_order(
        [buffer] + [swap(buffer, "col", n_col, 2 * k) for k in range(1, chips)], chip
    )
    buffer = in_order([buffer, swap(buffer, "col", n_col, 1)], core)
    buffer = buffer.transpose(1, 0, 2, 3).reshape(n_col, depth, width)
    left_tokens = buffer[:, share:].reshape(rows, width)
    weights = buffer[:, :share].reshape(share * n_col, width).astype(F32)

    token_rows = jnp.concatenate([left_tokens, right_tokens], axis=1)
    single_grad = dot(token_rows, proj_weight, 1, 1)
    in_grad = weights[: 2 * hid].reshape(2 * hid // width, width, width)
    in_grad = in_grad.transpose(1, 0, 2).reshape(width, 2 * hid)
    out_grad = weights[2 * hid : 3 * hid]
    head_rows = weights[3 * hid : 3 * hid + width // 2]
    head_grad = jnp.concatenate([head_rows[:, :bins], head_rows[:, bins:]], axis=0)
    return pair_grad, single_grad, in_grad, out_grad, head_grad


def solution(mesh):
    in_specs = (
        P("row", "col"),
        P("row", "col", None),
        P("col", None),
        P(),
        P(),
        P(),
        P(),
        P(),
        P(),
        P(),
        P("row", "col"),
        P(),
        P("row", None),
        P("row", "col"),
    )
    out_specs = (P("row", "col", None), P("row", "col"), P(), P(), P())
    return jax.shard_map(
        functools.partial(local, mesh.shape["row"], mesh.shape["col"]),
        mesh=mesh,
        in_specs=in_specs,
        out_specs=out_specs,
        check_vma=False,
    )
```

time: 519 us -> 112 us (0.22)
  the two profiles are of different devices: /device:TPU:0 before, /device:TPU:6 now
where the time goes in v1:
time: 112 us
  Pallas kernels  51.4 us (46%)
  starting transfers between devices  30 us (27%)
  blocking collectives  8.45 us (8%)
  local copies, waits for them, and re-layouts  7.96 us (7%)
  waiting for transfers between devices  7.85 us (7%)
  other arithmetic  3.94 us (4%)
    pallas_call x1, Pallas kernels, pair_grid(): pl.pallas_call(functools.partial(pair_kernel, tokens), grid_spec=grid_spe...  51.4 us
    ppermute x14, starting transfers between devices, swap(): return lax.ppermute(x, axis, [(i, i ^ mask) for i in range(size)])  18.9 us
    all_gather x1, blocking collectives, local(): joined = lax.all_gather(joined, 'col', axis=0, tiled=True)  8.45 us
    ppermute x1, starting transfers between devices, local(): lax.ppermute(own_half, ('row', 'col'), [(c // ratio * n_col + z * ratio +...  6.41 us
    ppermute x2, starting transfers between devices, local(): lax.ppermute(right_total, ('row', 'col'), [(z * n_col + c, c // ratio * n...  4.68 us
    ppermute x14, waiting for transfers between devices, swap(): return lax.ppermute(x, axis, [(i, i ^ mask) for i in range(size)])  4.32 us
    unnamed x9, local copies, waits for them, and re-layouts  4.22 us
    ppermute x2, waiting for transfers between devices, local(): lax.ppermute(right_total, ('row', 'col'), [(z * n_col + c, c // ratio * n...  3.52 us
  transfers between devices with their start and end apart: 17, of which 7 were waited for; matrix products, arithmetic and copies ran while one was open for 5% of the time, Pallas kernels for 0%

profile of v1, /device:TPU:6, one launch (start us, length us, event | category | flops | bytes accessed | tf_op | source)
XLA Modules:
  0.0 111.5 jit_solution(4683769699487705404)
XLA Ops:
  0.6 0.7 pad_maximum_fusion.4
  1.4 8.4 %all_gather.3 = bf16[384,384]{1,0:T(8,128)(2,1)S(1)} all-gather(bf16[48,384]{1,0:T(8,128)(2,1)S(1)} %pad_maximum_fusion.4), channel_id=1, replica_groups=mesh['row'=4,'col'=8] {'col'}, dimensions={0}, use_global_device_ids=true | all-gather | bytes 331776 | tf_op jit(solution)/shard_map/all_gather | solution.py:367
  9.8 0.2 fusion.5
  10.1 6.4 %collective-permute-start = (bf16[64,128]{1,0:T(8,128)(2,1)S(1)}, bf16[64,128]{1,0:T(8,128)(2,1)S(1)}, u32[]{:S(2)}, u32[]{:S(2)}) collective-permute-start(bf16[64,128]{1,0:T(8,128)(2,1)S(1)} %dynamic-slice_convert_fusion), channel_id=1, source_target_pairs={{0,0},{1,1},{8,2},{9,3},{16,4},{17,5},{24,6},{25,7},{2,8},{3,9},{1... | collective-permute-start | bytes 49160 | tf_op jit(solution)/shard_map/ppermute | solution.py:373
  16.5 0.6 slice.53.left_ref
  17.2 1.3 %reshape.52.perm_cols_ref = s32[8,64]{1,0:T(8,128)} reshape(s32[512]{0:T(512)} %param.25) | data formatting | bytes 4096 | tf_op jit(solution)/shard_map/reshape | solution.py:393
  18.5 1.4 %copy.25.head_ref = bf16[128,64]{1,0:T(8,128)(2,1)} copy(bf16[128,64]{0,1:T(8,128)(2,1)} %param.23) | data formatting | bytes 32768 | tf_op args[9]
  19.9 1.5 %copy.24.bins_ref = s32[128,64]{1,0:T(8,128)} copy(s32[128,64]{0,1:T(8,128)} %param.24) | data formatting | bytes 65536 | tf_op args[10]
  21.4 0.0 collective-permute-done.right_ref
  21.4 0.6 copy-done.2
  22.0 51.4 %shard_map.173 = (bf16[128,64,128]{2,1,0:T(8,128)(2,1)}, f32[128,128]{1,0:T(8,128)}, f32[64,128]{1,0:T(8,128)}, bf16[1664,128]{1,0:T(8,128)(2,1)}) custom-call(s32[1,8]{1,0:T(1,128)} %counts_ref.1, s32[1,256]{1,0:T(1,128)} %order_ref.1, bf16[128,64,128]{2,1,0:T(8,128)(2,1)} %pair_ref.1, f32[128,128]{1,0:T(8,128)} %slice.53.left_ref, ...), custom_call_target="tpu_custom_call" | custom-call | flops 17582522368 | bytes 4194304 | tf_op jit(solution)/shard_map/pallas_call | solution.py:298
  73.5 0.9 convert_element_type.76
  74.3 0.9 fusion.2
  75.3 0.1 collective-permute-start.1
  75.4 1.4 %collective-permute-done.1 = bf16[4,224,128]{2,1,0:T(8,128)(2,1)S(1)} collective-permute-done((bf16[4,224,128]{2,1,0:T(8,128)(2,1)S(1)}, bf16[4,224,128]{2,1,0:T(8,128)(2,1)S(1)}, u32[]{:S(2)}, u32[]{:S(2)}) %collective-permute-start.1) | collective-permute-done | bytes 229408 | tf_op jit(solution)/shard_map/ppermute | solution.py:319
  76.8 1.0 fusion
  77.9 0.1 collective-permute-start.2
  77.9 0.1 collective-permute-start.4
  78.0 3.4 %collective-permute-start.3 = (bf16[224,128]{1,0:T(8,128)(2,1)S(1)}, bf16[224,128]{1,0:T(8,128)(2,1)S(1)}, u32[]{:S(2)}, u32[]{:S(2)}) collective-permute-start(bf16[224,128]{1,0:T(8,128)(2,1)S(1)} %get-tuple-element.33), channel_id=1, source_target_pairs={{0,4},{1,5},{2,6},{3,7},{4,0},{5,1},{6,2},{7,3},{8,12},{9,13},{10,... | collective-permute-start | bytes 172040 | tf_op jit(solution)/shard_map/ppermute | solution.py:319
  81.4 1.1 collective-permute-done.2
  82.5 0.6 collective-permute-done.4
  83.1 1.0 collective-permute-done.3
  84.2 0.7 collective-permute-start.6
  84.9 1.3 %collective-permute-start.5 = (bf16[208,128]{1,0:T(8,128)(2,1)S(1)}, bf16[208,128]{1,0:T(8,128)(2,1)S(1)}, u32[]{:S(2)}, u32[]{:S(2)}) collective-permute-start(bf16[208,128]{1,0:T(8,128)(2,1)S(1)} %slice.55), channel_id=1, source_target_pairs={{0,8},{8,0},{16,24},{24,16},{1,9},{9,1},{17,25},{25,17},{2,10},{10... | collective-permute-start | bytes 159752 | tf_op jit(solution)/shard_map/ppermute | solution.py:319
  86.2 2.4 %collective-permute-start.7 = (bf16[208,128]{1,0:T(8,128)(2,1)S(1)}, bf16[208,128]{1,0:T(8,128)(2,1)S(1)}, u32[]{:S(2)}, u32[]{:S(2)}) collective-permute-start(bf16[208,128]{1,0:T(8,128)(2,1)S(1)} %slice.55), channel_id=1, source_target_pairs={{0,24},{8,16},{16,8},{24,0},{1,25},{9,17},{17,9},{25,1},{2,26},{10... | collective-permute-start | bytes 159752 | tf_op jit(solution)/shard_map/ppermute | solution.py:319
  88.6 2.0 %collective-permute-start.12 = (bf16[64,128]{1,0:T(8,128)(2,1)S(1)}, bf16[64,128]{1,0:T(8,128)(2,1)S(1)}, u32[]{:S(2)}, u32[]{:S(2)}) collective-permute-start(bf16[64,128]{1,0:T(8,128)(2,1)S(1)} %convert_element_type.92), channel_id=1, source_target_pairs={{0,8},{8,0},{16,24},{24,16},{1,9},{9,1},{17,25},{25,17},{2,10},{10... | collective-permute-start | bytes 49160 | tf_op jit(solution)/shard_map/ppermute | solution.py:319
  90.6 0.2 collective-permute-done.6
  90.8 2.2 %collective-permute-start.14 = (bf16[64,128]{1,0:T(8,128)(2,1)S(1)}, bf16[64,128]{1,0:T(8,128)(2,1)S(1)}, u32[]{:S(2)}, u32[]{:S(2)}) collective-permute-start(bf16[64,128]{1,0:T(8,128)(2,1)S(1)} %convert_element_type.92), channel_id=1, source_target_pairs={{0,24},{8,16},{16,8},{24,0},{1,25},{9,17},{17,9},{25,1},{2,26},{10... | collective-permute-start | bytes 49160 | tf_op jit(solution)/shard_map/ppermute | solution.py:319
  93.0 0.0 collective-permute-done.5
  93.0 0.0 collective-permute-done.7
  93.1 1.1 %collective-permute-start.10 = (bf16[224,128]{1,0:T(8,128)(2,1)S(1)}, bf16[224,128]{1,0:T(8,128)(2,1)S(1)}, u32[]{:S(2)}, u32[]{:S(2)}) collective-permute-start(bf16[224,128]{1,0:T(8,128)(2,1)S(1)} %pad_maximum_fusion.3), channel_id=1, source_target_pairs={{0,2},{1,3},{2,0},{3,1},{4,6},{5,7},{6,4},{7,5},{8,10},{9,11},{10,... | collective-permute-start | bytes 172040 | tf_op jit(solution)/shard_map/ppermute | solution.py:319
  94.2 0.9 collective-permute-start.9
  95.0 0.0 collective-permute-done.13
  95.0 1.6 %collective-permute-start.8 = (bf16[224,128]{1,0:T(8,128)(2,1)S(1)}, bf16[224,128]{1,0:T(8,128)(2,1)S(1)}, u32[]{:S(2)}, u32[]{:S(2)}) collective-permute-start(bf16[224,128]{1,0:T(8,128)(2,1)S(1)} %pad_maximum_fusion.3), channel_id=1, source_target_pairs={{0,6},{1,7},{2,4},{3,5},{4,2},{5,3},{6,0},{7,1},{8,14},{9,15},{10,... | collective-permute-start | bytes 172040 | tf_op jit(solution)/shard_map/ppermute | solution.py:319
  96.6 4.6 %collective-permute-start.16 = (bf16[64,128]{1,0:T(8,128)(2,1)S(1)}, bf16[64,128]{1,0:T(8,128)(2,1)S(1)}, u32[]{:S(2)}, u32[]{:S(2)}) collective-permute-start(bf16[64,128]{1,0:T(8,128)(2,1)S(1)} %add_convert_fusion.1), channel_id=1, source_target_pairs={{0,0},{1,1},{2,8},{3,9},{4,16},{5,17},{6,24},{7,25},{8,2},{9,3},{1... | collective-permute-start | bytes 49160 | tf_op jit(solution)/shard_map/ppermute | solution.py:409
  101.3 0.1 collective-permute-start.15
  101.4 0.1 select_bitcast_fusion.5
  101.5 3.1 %collective-permute-start.11 = (bf16[4,224,128]{2,1,0:T(8,128)(2,1)S(1)}, bf16[4,224,128]{2,1,0:T(8,128)(2,1)S(1)}, u32[]{:S(2)}, u32[]{:S(2)}) collective-permute-start(bf16[4,224,128]{2,1,0:T(8,128)(2,1)S(1)} %pad_maximum_fusion.1), channel_id=1, source_target_pairs={{0,1},{1,0},{2,3},{3,2},{4,5},{5,4},{6,7},{7,6},{8,9},{9,8},{10,11... | collective-permute-start | bytes 688136 | tf_op jit(solution)/shard_map/ppermute | solution.py:319
  104.6 1.3 %collective-permute-done.16 = bf16[64,128]{1,0:T(8,128)(2,1)S(1)} collective-permute-done((bf16[64,128]{1,0:T(8,128)(2,1)S(1)}, bf16[64,128]{1,0:T(8,128)(2,1)S(1)}, u32[]{:S(2)}, u32[]{:S(2)}) %collective-permute-start.16) | collective-permute-done | bytes 16416 | tf_op jit(solution)/shard_map/ppermute | solution.py:409
  105.9 2.2 %collective-permute-done.15 = bf16[64,128]{1,0:T(8,128)(2,1)S(1)} collective-permute-done((bf16[64,128]{1,0:T(8,128)(2,1)S(1)}, bf16[64,128]{1,0:T(8,128)(2,1)S(1)}, u32[]{:S(2)}, u32[]{:S(2)}) %collective-permute-start.15) | collective-permute-done | bytes 16416 | tf_op jit(solution)/shard_map/ppermute | solution.py:409
  108.1 0.1 select_bitcast_fusion.1
  108.3 0.0 copy-start.1
  108.3 0.1 bitcast_convert_fusion
  108.4 0.1 fusion.15
  108.5 0.7 slice.60
  109.2 0.7 copy.30
  109.9 0.8 copy.36
  110.8 0.8 fusion.10
  (29 shorter events, 0.3 us)
Async XLA Ops:
  10.1 11.3 %collective-permute-start = (bf16[64,128]{1,0:T(8,128)(2,1)S(1)}, bf16[64,128]{1,0:T(8,128)(2,1)S(1)}, u32[]{:S(2)}, u32[]{:S(2)}) collective-permute-start(bf16[64,128]{1,0:T(8,128)(2,1)S(1)} %dynamic-slice_convert_fusion), channel_id=1, source_target_pairs={{0,0},{1,1},{8,2},{9,3},{16,4},{17,5},{24,6},{25,7},{2,8},{3,9},{1... | collective-permute-start | bytes 49160 | tf_op jit(solution)/shard_map/ppermute | solution.py:373
  21.4 0.6 copy-start.2
  73.5 15.1 %copy-start = (f32[64,128]{1,0:T(8,128)S(1)}, f32[64,128]{1,0:T(8,128)}, u32[]{:S(2)}) copy-start(f32[64,128]{1,0:T(8,128)} %get-tuple-element.12) | copy-start | bytes 98308
  75.3 1.6 %collective-permute-start.1 = (bf16[4,224,128]{2,1,0:T(8,128)(2,1)S(1)}, bf16[4,224,128]{2,1,0:T(8,128)(2,1)S(1)}, u32[]{:S(2)}, u32[]{:S(2)}) collective-permute-start(bf16[4,224,128]{2,1,0:T(8,128)(2,1)S(1)} %fusion.2), channel_id=1, source_target_pairs={{0,1},{1,0},{2,3},{3,2},{4,5},{5,4},{6,7},{7,6},{8,9},{9,8},{10,11... | collective-permute-start | bytes 688136 | tf_op jit(solution)/shard_map/ppermute | solution.py:319
  77.9 4.6 %collective-permute-start.2 = (bf16[224,128]{1,0:T(8,128)(2,1)S(1)}, bf16[224,128]{1,0:T(8,128)(2,1)S(1)}, u32[]{:S(2)}, u32[]{:S(2)}) collective-permute-start(bf16[224,128]{1,0:T(8,128)(2,1)S(1)} %get-tuple-element.31), channel_id=1, source_target_pairs={{0,2},{1,3},{2,0},{3,1},{4,6},{5,7},{6,4},{7,5},{8,10},{9,11},{10,... | collective-permute-start | bytes 172040 | tf_op jit(solution)/shard_map/ppermute | solution.py:319
  77.9 5.2 %collective-permute-start.4 = (bf16[224,128]{1,0:T(8,128)(2,1)S(1)}, bf16[224,128]{1,0:T(8,128)(2,1)S(1)}, u32[]{:S(2)}, u32[]{:S(2)}) collective-permute-start(bf16[224,128]{1,0:T(8,128)(2,1)S(1)} %get-tuple-element.32), channel_id=1, source_target_pairs={{0,6},{1,7},{2,4},{3,5},{4,2},{5,3},{6,0},{7,1},{8,14},{9,15},{10,... | collective-permute-start | bytes 172040 | tf_op jit(solution)/shard_map/ppermute | solution.py:319
  78.0 6.1 %collective-permute-start.3 = (bf16[224,128]{1,0:T(8,128)(2,1)S(1)}, bf16[224,128]{1,0:T(8,128)(2,1)S(1)}, u32[]{:S(2)}, u32[]{:S(2)}) collective-permute-start(bf16[224,128]{1,0:T(8,128)(2,1)S(1)} %get-tuple-element.33), channel_id=1, source_target_pairs={{0,4},{1,5},{2,6},{3,7},{4,0},{5,1},{6,2},{7,3},{8,12},{9,13},{10,... | collective-permute-start | bytes 172040 | tf_op jit(solution)/shard_map/ppermute | solution.py:319
  84.2 6.6 %collective-permute-start.6 = (bf16[208,128]{1,0:T(8,128)(2,1)S(1)}, bf16[208,128]{1,0:T(8,128)(2,1)S(1)}, u32[]{:S(2)}, u32[]{:S(2)}) collective-permute-start(bf16[208,128]{1,0:T(8,128)(2,1)S(1)} %slice.55), channel_id=1, source_target_pairs={{0,16},{8,24},{16,0},{24,8},{1,17},{9,25},{17,1},{25,9},{2,18},{10... | collective-permute-start | bytes 159752 | tf_op jit(solution)/shard_map/ppermute | solution.py:319
  84.9 8.1 %collective-permute-start.5 = (bf16[208,128]{1,0:T(8,128)(2,1)S(1)}, bf16[208,128]{1,0:T(8,128)(2,1)S(1)}, u32[]{:S(2)}, u32[]{:S(2)}) collective-permute-start(bf16[208,128]{1,0:T(8,128)(2,1)S(1)} %slice.55), channel_id=1, source_target_pairs={{0,8},{8,0},{16,24},{24,16},{1,9},{9,1},{17,25},{25,17},{2,10},{10... | collective-permute-start | bytes 159752 | tf_op jit(solution)/shard_map/ppermute | solution.py:319
  86.2 6.8 %collective-permute-start.7 = (bf16[208,128]{1,0:T(8,128)(2,1)S(1)}, bf16[208,128]{1,0:T(8,128)(2,1)S(1)}, u32[]{:S(2)}, u32[]{:S(2)}) collective-permute-start(bf16[208,128]{1,0:T(8,128)(2,1)S(1)} %slice.55), channel_id=1, source_target_pairs={{0,24},{8,16},{16,8},{24,0},{1,25},{9,17},{17,9},{25,1},{2,26},{10... | collective-permute-start | bytes 159752 | tf_op jit(solution)/shard_map/ppermute | solution.py:319
  88.6 6.4 %collective-permute-start.13 = (bf16[64,128]{1,0:T(8,128)(2,1)S(1)}, bf16[64,128]{1,0:T(8,128)(2,1)S(1)}, u32[]{:S(2)}, u32[]{:S(2)}) collective-permute-start(bf16[64,128]{1,0:T(8,128)(2,1)S(1)} %convert_element_type.92), channel_id=1, source_target_pairs={{0,16},{8,24},{16,0},{24,8},{1,17},{9,25},{17,1},{25,9},{2,18},{10... | collective-permute-start | bytes 49160 | tf_op jit(solution)/shard_map/ppermute | solution.py:319
  88.6 8.0 %collective-permute-start.12 = (bf16[64,128]{1,0:T(8,128)(2,1)S(1)}, bf16[64,128]{1,0:T(8,128)(2,1)S(1)}, u32[]{:S(2)}, u32[]{:S(2)}) collective-permute-start(bf16[64,128]{1,0:T(8,128)(2,1)S(1)} %convert_element_type.92), channel_id=1, source_target_pairs={{0,8},{8,0},{16,24},{24,16},{1,9},{9,1},{17,25},{25,17},{2,10},{10... | collective-permute-start | bytes 49160 | tf_op jit(solution)/shard_map/ppermute | solution.py:319
  90.8 5.9 %collective-permute-start.14 = (bf16[64,128]{1,0:T(8,128)(2,1)S(1)}, bf16[64,128]{1,0:T(8,128)(2,1)S(1)}, u32[]{:S(2)}, u32[]{:S(2)}) collective-permute-start(bf16[64,128]{1,0:T(8,128)(2,1)S(1)} %convert_element_type.92), channel_id=1, source_target_pairs={{0,24},{8,16},{16,8},{24,0},{1,25},{9,17},{17,9},{25,1},{2,26},{10... | collective-permute-start | bytes 49160 | tf_op jit(solution)/shard_map/ppermute | solution.py:319
  93.1 8.3 %collective-permute-start.10 = (bf16[224,128]{1,0:T(8,128)(2,1)S(1)}, bf16[224,128]{1,0:T(8,128)(2,1)S(1)}, u32[]{:S(2)}, u32[]{:S(2)}) collective-permute-start(bf16[224,128]{1,0:T(8,128)(2,1)S(1)} %pad_maximum_fusion.3), channel_id=1, source_target_pairs={{0,2},{1,3},{2,0},{3,1},{4,6},{5,7},{6,4},{7,5},{8,10},{9,11},{10,... | collective-permute-start | bytes 172040 | tf_op jit(solution)/shard_map/ppermute | solution.py:319
  94.2 7.2 %collective-permute-start.9 = (bf16[224,128]{1,0:T(8,128)(2,1)S(1)}, bf16[224,128]{1,0:T(8,128)(2,1)S(1)}, u32[]{:S(2)}, u32[]{:S(2)}) collective-permute-start(bf16[224,128]{1,0:T(8,128)(2,1)S(1)} %pad_maximum_fusion.3), channel_id=1, source_target_pairs={{0,4},{1,5},{2,6},{3,7},{4,0},{5,1},{6,2},{7,3},{8,12},{9,13},{10,... | collective-permute-start | bytes 172040 | tf_op jit(solution)/shard_map/ppermute | solution.py:319
  95.0 6.3 %collective-permute-start.8 = (bf16[224,128]{1,0:T(8,128)(2,1)S(1)}, bf16[224,128]{1,0:T(8,128)(2,1)S(1)}, u32[]{:S(2)}, u32[]{:S(2)}) collective-permute-start(bf16[224,128]{1,0:T(8,128)(2,1)S(1)} %pad_maximum_fusion.3), channel_id=1, source_target_pairs={{0,6},{1,7},{2,4},{3,5},{4,2},{5,3},{6,0},{7,1},{8,14},{9,15},{10,... | collective-permute-start | bytes 172040 | tf_op jit(solution)/shard_map/ppermute | solution.py:319
  96.6 9.2 %collective-permute-start.16 = (bf16[64,128]{1,0:T(8,128)(2,1)S(1)}, bf16[64,128]{1,0:T(8,128)(2,1)S(1)}, u32[]{:S(2)}, u32[]{:S(2)}) collective-permute-start(bf16[64,128]{1,0:T(8,128)(2,1)S(1)} %add_convert_fusion.1), channel_id=1, source_target_pairs={{0,0},{1,1},{2,8},{3,9},{4,16},{5,17},{6,24},{7,25},{8,2},{9,3},{1... | collective-permute-start | bytes 49160 | tf_op jit(solution)/shard_map/ppermute | solution.py:409
  101.3 6.8 %collective-permute-start.15 = (bf16[64,128]{1,0:T(8,128)(2,1)S(1)}, bf16[64,128]{1,0:T(8,128)(2,1)S(1)}, u32[]{:S(2)}, u32[]{:S(2)}) collective-permute-start(bf16[64,128]{1,0:T(8,128)(2,1)S(1)} %add_convert_fusion.1), channel_id=1, source_target_pairs={{0,1},{1,0},{2,9},{3,8},{4,17},{5,16},{6,25},{7,24},{8,3},{9,2},{1... | collective-permute-start | bytes 49160 | tf_op jit(solution)/shard_map/ppermute | solution.py:409
  101.5 6.6 %collective-permute-start.11 = (bf16[4,224,128]{2,1,0:T(8,128)(2,1)S(1)}, bf16[4,224,128]{2,1,0:T(8,128)(2,1)S(1)}, u32[]{:S(2)}, u32[]{:S(2)}) collective-permute-start(bf16[4,224,128]{2,1,0:T(8,128)(2,1)S(1)} %pad_maximum_fusion.1), channel_id=1, source_target_pairs={{0,1},{1,0},{2,3},{3,2},{4,5},{5,4},{6,7},{7,6},{8,9},{9,8},{10,11... | collective-permute-start | bytes 688136 | tf_op jit(solution)/shard_map/ppermute | solution.py:319
  108.3 2.5 %copy-start.1 = (bf16[48,256]{1,0:T(8,128)(2,1)S(1)}, bf16[48,256]{1,0:T(8,128)(2,1)}, u32[]{:S(2)}) copy-start(bf16[48,256]{1,0:T(8,128)(2,1)} %param.16) | copy-start | bytes 73732

commit v2 on v1

--- a/solution.py
+++ b/solution.py
@@ -8,6 +8,7 @@
 from jax.sharding import PartitionSpec as P
 
 TILE = 32
+LANES = 128
 BLOCK_ROWS = 32
 CHUNK = 256
 F32 = jnp.float32
@@ -24,25 +25,25 @@
 
 
 def norm(field):
-    centred = field - jnp.mean(field, axis=-1, keepdims=True)
-    scaling = lax.rsqrt(jnp.mean(centred * centred, axis=-1, keepdims=True) + 1e-05)
+    centred = field - jnp.mean(field, axis=0, keepdims=True)
+    scaling = lax.rsqrt(jnp.mean(centred * centred, axis=0, keepdims=True) + 1e-05)
     return centred * scaling, scaling
 
 
-def forward(inputs, w_in, w_out, act_ref, slope_ref, hidden_ref):
-    hid = w_out.shape[0]
+def forward(inputs, in_turned, out_turned, act_ref, slope_ref, hidden_ref):
+    hid = out_turned.shape[1]
     result = None
     for j in range(0, hid, CHUNK):
-        half_gate = dot(inputs, w_in[:, j : j + CHUNK])
-        up = dot(inputs, w_in[:, hid + j : hid + j + CHUNK])
+        half_gate = dot(in_turned[j : j + CHUNK, :], inputs).astype(BF16)
+        up = dot(in_turned[hid + j : hid + j + CHUNK, :], inputs).astype(BF16)
         twice_sig = 1.0 + jnp.tanh(half_gate)
         act = half_gate * twice_sig
-        hidden = (act * up).astype(BF16)
-        act_ref[:, j : j + CHUNK] = act
-        slope_ref[:, j : j + CHUNK] = up * (twice_sig + act * (2.0 - twice_sig))
+        hidden = act * up
+        act_ref[j : j + CHUNK, :] = act
+        slope_ref[j : j + CHUNK, :] = up * (twice_sig + act * (2.0 - twice_sig))
         if hidden_ref is not None:
-            hidden_ref[:, j : j + CHUNK] = hidden
-        part = dot(hidden, w_out[j : j + CHUNK, :])
+            hidden_ref[j : j + CHUNK, :] = hidden
+        part = dot(out_turned[:, j : j + CHUNK], hidden)
         result = part if result is None else result + part
     return result
 
@@ -51,19 +52,23 @@
     hid = w_out.shape[0]
     grad_normed = None
     for j in range(0, hid, CHUNK):
-        grad_hidden = dot(grad_out, w_out[j : j + CHUNK, :], 1, 1)
-        grad_gate = (grad_hidden * slope_ref[:, j : j + CHUNK]).astype(BF16)
-        grad_up = (grad_hidden * act_ref[:, j : j + CHUNK]).astype(BF16)
+        grad_hidden = dot(w_out[j : j + CHUNK, :], grad_out).astype(BF16)
+        grad_gate = grad_hidden * slope_ref[j : j + CHUNK, :]
+        grad_up = grad_hidden * act_ref[j : j + CHUNK, :]
         if both_ref is not None:
-            both_ref[:, j : j + CHUNK] = grad_gate
-            both_ref[:, hid + j : hid + j + CHUNK] = grad_up
-        part = dot(grad_gate, w_in[:, j : j + CHUNK], 1, 1)
-        part = part + dot(grad_up, w_in[:, hid + j : hid + j + CHUNK], 1, 1)
+            both_ref[j : j + CHUNK, :] = grad_gate
+            both_ref[hid + j : hid + j + CHUNK, :] = grad_up
+        part = dot(w_in[:, j : j + CHUNK], grad_gate)
+        part = part + dot(w_in[:, hid + j : hid + j + CHUNK], grad_up)
         grad_normed = part if grad_normed is None else grad_normed + part
     grad_normed = grad_normed * gain
-    mean = jnp.mean(grad_normed, axis=-1, keepdims=True)
-    slant = jnp.mean(grad_normed * normed, axis=-1, keepdims=True)
+    mean = jnp.mean(grad_normed, axis=0, keepdims=True)
+    slant = jnp.mean(grad_normed * normed, axis=0, keepdims=True)
     return scaling * (grad_normed - mean - normed * slant)
+
+
+def turned(x):
+    return jnp.transpose(x.astype(F32)).astype(x.dtype)
 
 
 def pair_kernel(
@@ -89,8 +94,15 @@
     weights_ref,
     live_ref,
     target_ref,
+    rows_ref,
+    gains_ref,
     first_half,
     second_half,
+    first_in_turned,
+    second_in_turned,
+    first_out_turned,
+    second_out_turned,
+    head_turned,
     act_one,
     slope_one,
     act_two,
@@ -104,9 +116,9 @@
     block_rows, cols, width = pair_ref.shape
     pairs = block_rows * cols
     hid = first_out_ref.shape[0]
-    tiles = pairs // TILE
     step = pl.program_id(0)
-    blocks = target_ref.shape[0]
+    group = LANES // cols
+    vectors = pairs // LANES
 
     @pl.when(step == 0)
     def _():
@@ -114,9 +126,18 @@
         in_sum[...] = jnp.zeros_like(in_sum)
         out_sum[...] = jnp.zeros_like(out_sum)
         head_sum[...] = jnp.zeros_like(head_sum)
-        for half, whole in ((first_half, first_in_ref), (second_half, second_in_ref)):
+        for half, half_turned, whole in (
+            (first_half, first_in_turned, first_in_ref),
+            (second_half, second_in_turned, second_in_ref),
+        ):
             half[:, :hid] = whole[:, :hid] * jnp.asarray(0.5, BF16)
             half[:, hid:] = whole[:, hid:]
+            half_turned[...] = turned(half[...])
+        first_out_turned[...] = turned(first_out_ref[...])
+        second_out_turned[...] = turned(second_out_ref[...])
+        head_turned[...] = turned(head_ref[...])
+        gains_ref[:, 0:1] = jnp.transpose(gain_first_ref[...])
+        gains_ref[:, 1:2] = jnp.transpose(gain_second_ref[...])
         count = counts_ref[0, lax.axis_index("col")]
 
         def place(t, carry):
@@ -131,70 +152,76 @@
         pick_rows = (lax.broadcasted_iota(jnp.int32, (rows, rows), 0) == perm_rows).astype(BF16)
         pick_cols = (lax.broadcasted_iota(jnp.int32, (cols, cols), 0) == perm_cols).astype(BF16)
         bins = bins_ref[...].astype(F32).astype(BF16)
-        moved = dot(bins, pick_rows, 0, 0).astype(BF16)
-        moved = dot(pick_cols, moved, 0, 0)
-        for b in range(blocks):
-            target_ref[b] = moved[:, b * block_rows : (b + 1) * block_rows].astype(jnp.int32)
+        moved = dot(pick_rows, bins, 0, 0).astype(BF16)
+        rows_ref[...] = dot(moved, pick_cols)
+        target_ref[...] = jnp.concatenate(
+            [rows_ref[pl.ds(k, rows // group, stride=group), :] for k in range(group)], axis=1
+        )
 
     field = pair_ref[...].astype(F32) + left_ref[...][:, None, :]
     field = (field + right_ref[...].astype(F32)[None]).reshape(pairs, width)
+    field = jnp.transpose(field)
     normed_one, scaling_one = norm(field)
-    inputs_one = (normed_one * gain_first_ref[...]).astype(BF16)
-    delta_one = forward(inputs_one, first_half, first_out_ref, act_one, slope_one, None)
+    inputs_one = (normed_one * gains_ref[:, 0:1]).astype(BF16)
+    delta_one = forward(inputs_one, first_in_turned, first_out_turned, act_one, slope_one, None)
     pair_one = (field + delta_one).astype(BF16).astype(F32)
 
     normed_two, scaling_two = norm(pair_one)
-    inputs_two = (normed_two * gain_second_ref[...]).astype(BF16)
-    delta_two = forward(inputs_two, second_half, second_out_ref, act_two, slope_two, hidden_two)
-    live = [live_ref[step * tiles + t] for t in range(tiles)]
-
-    def masked(x):
-        return jnp.concatenate(
-            [x[t * TILE : (t + 1) * TILE] * live[t] for t in range(tiles)], axis=0
-        )
-
-    pair_two = (pair_one + masked(delta_two)).astype(BF16)
-
-    logits = dot(pair_two, head_ref[...])
-    exponent = jnp.exp(logits - jnp.max(logits, axis=-1, keepdims=True))
-    probability = exponent * (1.0 / jnp.sum(exponent, axis=-1, keepdims=True))
-    target = target_ref[step]
-    bin_ids = lax.broadcasted_iota(jnp.int32, (cols, logits.shape[-1]), 1)
-    onehot = jnp.concatenate(
-        [(target[:, r : r + 1] == bin_ids).astype(F32) for r in range(block_rows)], axis=0
-    )
-    grad_logits = (probability - onehot).astype(BF16)
-    grad_two = dot(grad_logits, head_ref[...], 1, 1).astype(BF16).astype(F32)
-    head_sum[...] += dot(pair_two, grad_logits, 0, 0)
-
-    grad_delta = masked(grad_two).astype(BF16)
+    inputs_two = (normed_two * gains_ref[:, 1:2]).astype(BF16)
+    delta_two = forward(
+        inputs_two, second_in_turned, second_out_turned, act_two, slope_two, hidden_two
+    )
+    lane_tile = lax.broadcasted_iota(jnp.int32, (1, LANES), 1) // TILE
+    tiles = LANES // TILE
+    live_parts = []
+    for k in range(vectors):
+        first_tile = (step * vectors + k) * tiles
+        part = jnp.full((1, LANES), live_ref[first_tile], F32)
+        for t in range(1, tiles):
+            part = jnp.where(lane_tile == t, live_ref[first_tile + t], part)
+        live_parts.append(part)
+    live = jnp.concatenate(live_parts, axis=1)
+    pair_two = (pair_one + live * delta_two).astype(BF16)
+
+    logits = dot(head_turned[...], pair_two)
+    exponent = jnp.exp(logits - jnp.max(logits, axis=0, keepdims=True))
+    probability = exponent * (1.0 / jnp.sum(exponent, axis=0, keepdims=True))
+    target = jnp.concatenate(
+        [target_ref[pl.ds(step * vectors + k, 1), :] for k in range(vectors)], axis=1
+    ).astype(jnp.int32)
+    onehot = lax.broadcasted_iota(jnp.int32, logits.shape, 0) == target
+    grad_logits = (probability - onehot.astype(F32)).astype(BF16)
+    grad_two = dot(head_ref[...], grad_logits).astype(BF16).astype(F32)
+    head_sum[...] += dot(pair_two, grad_logits, 1, 1)
+
+    grad_delta = (grad_two * live).astype(BF16)
     back_two = backward(
         grad_delta,
         normed_two,
         scaling_two,
-        gain_second_ref[...],
+        gains_ref[:, 1:2],
         second_half,
         second_out_ref,
         act_two,
         slope_two,
         both_two,
     )
-    in_sum[...] += dot(inputs_two, both_two[...], 0, 0)
-    out_sum[...] += dot(grad_delta, hidden_two[...], 0, 0)
+    in_sum[...] += dot(inputs_two, both_two[...], 1, 1)
+    out_sum[...] += dot(grad_delta, hidden_two[...], 1, 1)
 
     grad_one = (grad_two + back_two).astype(BF16)
     back_one = backward(
         grad_one,
         normed_one,
         scaling_one,
-        gain_first_ref[...],
+        gains_ref[:, 0:1],
         first_half,
         first_out_ref,
         act_one,
         slope_one,
         None,
     )
-    grad_zero = (grad_one.astype(F32) + back_one).reshape(block_rows, cols, width)
+    grad_zero = jnp.transpose(grad_one.astype(F32) + back_one).reshape(block_rows, cols, width)
     pair_grad_ref[...] = grad_zero.astype(BF16)
     left_grad_ref[...] = jnp.sum(grad_zero, axis=1)
     right_grad_ref[...] += jnp.sum(grad_zero, axis=0)
@@ -280,15 +307,22 @@
         ],
         scratch_shapes=[
             pltpu.SMEM((rows * cols // TILE,), F32),
-            pltpu.VMEM((rows // block_rows, cols, block_rows), jnp.int32),
+            pltpu.VMEM((rows * cols // LANES, LANES), F32),
+            pltpu.VMEM((rows, cols), F32),
+            pltpu.VMEM((width, 2), F32),
             pltpu.VMEM((width, 2 * hid), BF16),
             pltpu.VMEM((width, 2 * hid), BF16),
-            pltpu.VMEM((pairs, hid), F32),
-            pltpu.VMEM((pairs, hid), F32),
-            pltpu.VMEM((pairs, hid), F32),
-            pltpu.VMEM((pairs, hid), F32),
-            pltpu.VMEM((pairs, hid), BF16),
-            pltpu.VMEM((pairs, 2 * hid), BF16),
+            pltpu.VMEM((2 * hid, width), BF16),
+            pltpu.VMEM((2 * hid, width), BF16),
+            pltpu.VMEM((width, hid), BF16),
+            pltpu.VMEM((width, hid), BF16),
+            pltpu.VMEM((bins, width), BF16),
+            pltpu.VMEM((hid, pairs), BF16),
+            pltpu.VMEM((hid, pairs), BF16),
+            pltpu.VMEM((hid, pairs), BF16),
+            pltpu.VMEM((hid, pairs), BF16),
+            pltpu.VMEM((hid, pairs), BF16),
+            pltpu.VMEM((2 * hid, pairs), BF16),
             pltpu.VMEM((width, 2 * hid), F32),
             pltpu.VMEM((width, hid), F32),
             pltpu.VMEM((width, bins), F32),

time: 112 us -> 101 us (0.902)
  Pallas kernels: 51.4 us -> 40.4 us
    pallas_call x1, Pallas kernels: 51.4 us -> 40.4 us  [pair_grid(): pl.pallas_call(functools.partial(pair_kernel, tokens), grid_spec=grid_spe...]
where the time goes in v2:
time: 101 us; the launch traced here: 100 us
  Pallas kernels  40.4 us (40%)
  starting transfers between devices  30 us (30%)
  blocking collectives  8.45 us (8%)
  local copies, waits for them, and re-layouts  7.96 us (8%)
  waiting for transfers between devices  7.85 us (8%)
  other arithmetic  3.94 us (4%)
    pallas_call x1, Pallas kernels, pair_grid(): pl.pallas_call(functools.partial(pair_kernel, tokens), grid_spec=grid_spe...  40.4 us
    ppermute x14, starting transfers between devices, swap(): return lax.ppermute(x, axis, [(i, i ^ mask) for i in range(size)])  18.9 us
    all_gather x1, blocking collectives, local(): joined = lax.all_gather(joined, 'col', axis=0, tiled=True)  8.45 us
    ppermute x1, starting transfers between devices, local(): lax.ppermute(own_half, ('row', 'col'), [(c // ratio * n_col + z * ratio +...  6.41 us
    ppermute x2, starting transfers between devices, local(): lax.ppermute(right_total, ('row', 'col'), [(z * n_col + c, c // ratio * n...  4.68 us
    ppermute x14, waiting for transfers between devices, swap(): return lax.ppermute(x, axis, [(i, i ^ mask) for i in range(size)])  4.32 us
    unnamed x9, local copies, waits for them, and re-layouts  4.22 us
    ppermute x2, waiting for transfers between devices, local(): lax.ppermute(right_total, ('row', 'col'), [(z * n_col + c, c // ratio * n...  3.52 us
  transfers between devices with their start and end apart: 17, of which 7 were waited for; matrix products, arithmetic and copies ran while one was open for 5% of the time, Pallas kernels for 0%

profile of v2, /device:TPU:6, one launch (start us, length us, event | category | flops | bytes accessed | tf_op | source)
XLA Modules:
  0.0 100.5 jit_solution(12776193606958739640)
XLA Ops:
  0.6 0.7 pad_maximum_fusion.4
  1.4 8.4 %all_gather.3 = bf16[384,384]{1,0:T(8,128)(2,1)S(1)} all-gather(bf16[48,384]{1,0:T(8,128)(2,1)S(1)} %pad_maximum_fusion.4), channel_id=1, replica_groups=mesh['row'=4,'col'=8] {'col'}, dimensions={0}, use_global_device_ids=true | all-gather | bytes 331776 | tf_op jit(solution)/shard_map/all_gather | solution.py:401
  9.8 0.2 fusion.5
  10.1 6.4 %collective-permute-start = (bf16[64,128]{1,0:T(8,128)(2,1)S(1)}, bf16[64,128]{1,0:T(8,128)(2,1)S(1)}, u32[]{:S(2)}, u32[]{:S(2)}) collective-permute-start(bf16[64,128]{1,0:T(8,128)(2,1)S(1)} %dynamic-slice_convert_fusion), channel_id=1, source_target_pairs={{0,0},{1,1},{8,2},{9,3},{16,4},{17,5},{24,6},{25,7},{2,8},{3,9},{1... | collective-permute-start | bytes 49160 | tf_op jit(solution)/shard_map/ppermute | solution.py:407
  16.5 0.6 slice.53.left_ref
  17.2 1.3 %reshape.52.perm_cols_ref = s32[8,64]{1,0:T(8,128)} reshape(s32[512]{0:T(512)} %param.25) | data formatting | bytes 4096 | tf_op jit(solution)/shard_map/reshape | solution.py:427
  18.5 1.4 %copy.25.head_ref = bf16[128,64]{1,0:T(8,128)(2,1)} copy(bf16[128,64]{0,1:T(8,128)(2,1)} %param.23) | data formatting | bytes 32768 | tf_op args[9]
  19.9 1.5 %copy.24.bins_ref = s32[128,64]{1,0:T(8,128)} copy(s32[128,64]{0,1:T(8,128)} %param.24) | data formatting | bytes 65536 | tf_op args[10]
  21.4 0.0 collective-permute-done.right_ref
  21.4 0.6 copy-done.2
  22.0 40.4 %shard_map.173 = (bf16[128,64,128]{2,1,0:T(8,128)(2,1)}, f32[128,128]{1,0:T(8,128)}, f32[64,128]{1,0:T(8,128)}, bf16[1664,128]{1,0:T(8,128)(2,1)}) custom-call(s32[1,8]{1,0:T(1,128)} %counts_ref.1, s32[1,256]{1,0:T(1,128)} %order_ref.1, bf16[128,64,128]{2,1,0:T(8,128)(2,1)} %pair_ref.1, f32[128,128]{1,0:T(8,128)} %slice.53.left_ref, ...), custom_call_target="tpu_custom_call" | custom-call | flops 17582522368 | bytes 4194304 | tf_op jit(solution)/shard_map/pallas_call | solution.py:332
  62.4 0.9 convert_element_type.76
  63.3 0.9 fusion.2
  64.2 0.1 collective-permute-start.1
  64.3 1.4 %collective-permute-done.1 = bf16[4,224,128]{2,1,0:T(8,128)(2,1)S(1)} collective-permute-done((bf16[4,224,128]{2,1,0:T(8,128)(2,1)S(1)}, bf16[4,224,128]{2,1,0:T(8,128)(2,1)S(1)}, u32[]{:S(2)}, u32[]{:S(2)}) %collective-permute-start.1) | collective-permute-done | bytes 229408 | tf_op jit(solution)/shard_map/ppermute | solution.py:353
  65.8 1.0 fusion
  66.8 0.1 collective-permute-start.2
  66.9 0.1 collective-permute-start.4
  66.9 3.4 %collective-permute-start.3 = (bf16[224,128]{1,0:T(8,128)(2,1)S(1)}, bf16[224,128]{1,0:T(8,128)(2,1)S(1)}, u32[]{:S(2)}, u32[]{:S(2)}) collective-permute-start(bf16[224,128]{1,0:T(8,128)(2,1)S(1)} %get-tuple-element.33), channel_id=1, source_target_pairs={{0,4},{1,5},{2,6},{3,7},{4,0},{5,1},{6,2},{7,3},{8,12},{9,13},{10,... | collective-permute-start | bytes 172040 | tf_op jit(solution)/shard_map/ppermute | solution.py:353
  70.3 1.1 %collective-permute-done.2 = bf16[224,128]{1,0:T(8,128)(2,1)S(1)} collective-permute-done((bf16[224,128]{1,0:T(8,128)(2,1)S(1)}, bf16[224,128]{1,0:T(8,128)(2,1)S(1)}, u32[]{:S(2)}, u32[]{:S(2)}) %collective-permute-start.2) | collective-permute-done | bytes 57376 | tf_op jit(solution)/shard_map/ppermute | solution.py:353
  71.4 0.6 collective-permute-done.4
  72.1 1.0 collective-permute-done.3
  73.1 0.7 collective-permute-start.6
  73.8 1.3 %collective-permute-start.5 = (bf16[208,128]{1,0:T(8,128)(2,1)S(1)}, bf16[208,128]{1,0:T(8,128)(2,1)S(1)}, u32[]{:S(2)}, u32[]{:S(2)}) collective-permute-start(bf16[208,128]{1,0:T(8,128)(2,1)S(1)} %slice.55), channel_id=1, source_target_pairs={{0,8},{8,0},{16,24},{24,16},{1,9},{9,1},{17,25},{25,17},{2,10},{10... | collective-permute-start | bytes 159752 | tf_op jit(solution)/shard_map/ppermute | solution.py:353
  75.1 2.4 %collective-permute-start.7 = (bf16[208,128]{1,0:T(8,128)(2,1)S(1)}, bf16[208,128]{1,0:T(8,128)(2,1)S(1)}, u32[]{:S(2)}, u32[]{:S(2)}) collective-permute-start(bf16[208,128]{1,0:T(8,128)(2,1)S(1)} %slice.55), channel_id=1, source_target_pairs={{0,24},{8,16},{16,8},{24,0},{1,25},{9,17},{17,9},{25,1},{2,26},{10... | collective-permute-start | bytes 159752 | tf_op jit(solution)/shard_map/ppermute | solution.py:353
  77.5 0.0 collective-permute-start.13
  77.5 2.0 %collective-permute-start.12 = (bf16[64,128]{1,0:T(8,128)(2,1)S(1)}, bf16[64,128]{1,0:T(8,128)(2,1)S(1)}, u32[]{:S(2)}, u32[]{:S(2)}) collective-permute-start(bf16[64,128]{1,0:T(8,128)(2,1)S(1)} %convert_element_type.92), channel_id=1, source_target_pairs={{0,8},{8,0},{16,24},{24,16},{1,9},{9,1},{17,25},{25,17},{2,10},{10... | collective-permute-start | bytes 49160 | tf_op jit(solution)/shard_map/ppermute | solution.py:353
  79.5 0.2 collective-permute-done.6
  79.7 2.2 %collective-permute-start.14 = (bf16[64,128]{1,0:T(8,128)(2,1)S(1)}, bf16[64,128]{1,0:T(8,128)(2,1)S(1)}, u32[]{:S(2)}, u32[]{:S(2)}) collective-permute-start(bf16[64,128]{1,0:T(8,128)(2,1)S(1)} %convert_element_type.92), channel_id=1, source_target_pairs={{0,24},{8,16},{16,8},{24,0},{1,25},{9,17},{17,9},{25,1},{2,26},{10... | collective-permute-start | bytes 49160 | tf_op jit(solution)/shard_map/ppermute | solution.py:353
  82.0 1.1 %collective-permute-start.10 = (bf16[224,128]{1,0:T(8,128)(2,1)S(1)}, bf16[224,128]{1,0:T(8,128)(2,1)S(1)}, u32[]{:S(2)}, u32[]{:S(2)}) collective-permute-start(bf16[224,128]{1,0:T(8,128)(2,1)S(1)} %pad_maximum_fusion.3), channel_id=1, source_target_pairs={{0,2},{1,3},{2,0},{3,1},{4,6},{5,7},{6,4},{7,5},{8,10},{9,11},{10,... | collective-permute-start | bytes 172040 | tf_op jit(solution)/shard_map/ppermute | solution.py:353
  83.1 0.9 collective-permute-start.9
  84.0 0.0 collective-permute-done.13
  84.0 1.6 %collective-permute-start.8 = (bf16[224,128]{1,0:T(8,128)(2,1)S(1)}, bf16[224,128]{1,0:T(8,128)(2,1)S(1)}, u32[]{:S(2)}, u32[]{:S(2)}) collective-permute-start(bf16[224,128]{1,0:T(8,128)(2,1)S(1)} %pad_maximum_fusion.3), channel_id=1, source_target_pairs={{0,6},{1,7},{2,4},{3,5},{4,2},{5,3},{6,0},{7,1},{8,14},{9,15},{10,... | collective-permute-start | bytes 172040 | tf_op jit(solution)/shard_map/ppermute | solution.py:353
  85.6 4.6 %collective-permute-start.16 = (bf16[64,128]{1,0:T(8,128)(2,1)S(1)}, bf16[64,128]{1,0:T(8,128)(2,1)S(1)}, u32[]{:S(2)}, u32[]{:S(2)}) collective-permute-start(bf16[64,128]{1,0:T(8,128)(2,1)S(1)} %add_convert_fusion.1), channel_id=1, source_target_pairs={{0,0},{1,1},{2,8},{3,9},{4,16},{5,17},{6,24},{7,25},{8,2},{9,3},{1... | collective-permute-start | bytes 49160 | tf_op jit(solution)/shard_map/ppermute | solution.py:443
  90.2 0.1 collective-permute-start.15
  90.3 0.0 collective-permute-done.10
  90.3 0.1 select_bitcast_fusion.5
  90.4 3.1 %collective-permute-start.11 = (bf16[4,224,128]{2,1,0:T(8,128)(2,1)S(1)}, bf16[4,224,128]{2,1,0:T(8,128)(2,1)S(1)}, u32[]{:S(2)}, u32[]{:S(2)}) collective-permute-start(bf16[4,224,128]{2,1,0:T(8,128)(2,1)S(1)} %pad_maximum_fusion.1), channel_id=1, source_target_pairs={{0,1},{1,0},{2,3},{3,2},{4,5},{5,4},{6,7},{7,6},{8,9},{9,8},{10,11... | collective-permute-start | bytes 688136 | tf_op jit(solution)/shard_map/ppermute | solution.py:353
  93.5 1.3 %collective-permute-done.16 = bf16[64,128]{1,0:T(8,128)(2,1)S(1)} collective-permute-done((bf16[64,128]{1,0:T(8,128)(2,1)S(1)}, bf16[64,128]{1,0:T(8,128)(2,1)S(1)}, u32[]{:S(2)}, u32[]{:S(2)}) %collective-permute-start.16) | collective-permute-done | bytes 16416 | tf_op jit(solution)/shard_map/ppermute | solution.py:443
  94.8 2.2 %collective-permute-done.15 = bf16[64,128]{1,0:T(8,128)(2,1)S(1)} collective-permute-done((bf16[64,128]{1,0:T(8,128)(2,1)S(1)}, bf16[64,128]{1,0:T(8,128)(2,1)S(1)}, u32[]{:S(2)}, u32[]{:S(2)}) %collective-permute-start.15) | collective-permute-done | bytes 16416 | tf_op jit(solution)/shard_map/ppermute | solution.py:443
  97.0 0.1 select_bitcast_fusion.1
  97.2 0.0 copy-start.1
  97.2 0.1 bitcast_convert_fusion
  97.3 0.1 fusion.15
  97.4 0.7 slice.60
  98.2 0.7 copy.30
  98.9 0.8 copy.36
  99.7 0.8 fusion.10
  (29 shorter events, 0.3 us)
Async XLA Ops:
  10.1 11.3 %collective-permute-start = (bf16[64,128]{1,0:T(8,128)(2,1)S(1)}, bf16[64,128]{1,0:T(8,128)(2,1)S(1)}, u32[]{:S(2)}, u32[]{:S(2)}) collective-permute-start(bf16[64,128]{1,0:T(8,128)(2,1)S(1)} %dynamic-slice_convert_fusion), channel_id=1, source_target_pairs={{0,0},{1,1},{8,2},{9,3},{16,4},{17,5},{24,6},{25,7},{2,8},{3,9},{1... | collective-permute-start | bytes 49160 | tf_op jit(solution)/shard_map/ppermute | solution.py:407
  21.4 0.6 copy-start.2
  62.4 15.1 %copy-start = (f32[64,128]{1,0:T(8,128)S(1)}, f32[64,128]{1,0:T(8,128)}, u32[]{:S(2)}) copy-start(f32[64,128]{1,0:T(8,128)} %get-tuple-element.12) | copy-start | bytes 98308
  64.2 1.6 %collective-permute-start.1 = (bf16[4,224,128]{2,1,0:T(8,128)(2,1)S(1)}, bf16[4,224,128]{2,1,0:T(8,128)(2,1)S(1)}, u32[]{:S(2)}, u32[]{:S(2)}) collective-permute-start(bf16[4,224,128]{2,1,0:T(8,128)(2,1)S(1)} %fusion.2), channel_id=1, source_target_pairs={{0,1},{1,0},{2,3},{3,2},{4,5},{5,4},{6,7},{7,6},{8,9},{9,8},{10,11... | collective-permute-start | bytes 688136 | tf_op jit(solution)/shard_map/ppermute | solution.py:353
  66.8 4.6 %collective-permute-start.2 = (bf16[224,128]{1,0:T(8,128)(2,1)S(1)}, bf16[224,128]{1,0:T(8,128)(2,1)S(1)}, u32[]{:S(2)}, u32[]{:S(2)}) collective-permute-start(bf16[224,128]{1,0:T(8,128)(2,1)S(1)} %get-tuple-element.31), channel_id=1, source_target_pairs={{0,2},{1,3},{2,0},{3,1},{4,6},{5,7},{6,4},{7,5},{8,10},{9,11},{10,... | collective-permute-start | bytes 172040 | tf_op jit(solution)/shard_map/ppermute | solution.py:353
  66.9 5.2 %collective-permute-start.4 = (bf16[224,128]{1,0:T(8,128)(2,1)S(1)}, bf16[224,128]{1,0:T(8,128)(2,1)S(1)}, u32[]{:S(2)}, u32[]{:S(2)}) collective-permute-start(bf16[224,128]{1,0:T(8,128)(2,1)S(1)} %get-tuple-element.32), channel_id=1, source_target_pairs={{0,6},{1,7},{2,4},{3,5},{4,2},{5,3},{6,0},{7,1},{8,14},{9,15},{10,... | collective-permute-start | bytes 172040 | tf_op jit(solution)/shard_map/ppermute | solution.py:353
  66.9 6.1 %collective-permute-start.3 = (bf16[224,128]{1,0:T(8,128)(2,1)S(1)}, bf16[224,128]{1,0:T(8,128)(2,1)S(1)}, u32[]{:S(2)}, u32[]{:S(2)}) collective-permute-start(bf16[224,128]{1,0:T(8,128)(2,1)S(1)} %get-tuple-element.33), channel_id=1, source_target_pairs={{0,4},{1,5},{2,6},{3,7},{4,0},{5,1},{6,2},{7,3},{8,12},{9,13},{10,... | collective-permute-start | bytes 172040 | tf_op jit(solution)/shard_map/ppermute | solution.py:353
  73.1 6.6 %collective-permute-start.6 = (bf16[208,128]{1,0:T(8,128)(2,1)S(1)}, bf16[208,128]{1,0:T(8,128)(2,1)S(1)}, u32[]{:S(2)}, u32[]{:S(2)}) collective-permute-start(bf16[208,128]{1,0:T(8,128)(2,1)S(1)} %slice.55), channel_id=1, source_target_pairs={{0,16},{8,24},{16,0},{24,8},{1,17},{9,25},{17,1},{25,9},{2,18},{10... | collective-permute-start | bytes 159752 | tf_op jit(solution)/shard_map/ppermute | solution.py:353
  73.8 8.1 %collective-permute-start.5 = (bf16[208,128]{1,0:T(8,128)(2,1)S(1)}, bf16[208,128]{1,0:T(8,128)(2,1)S(1)}, u32[]{:S(2)}, u32[]{:S(2)}) collective-permute-start(bf16[208,128]{1,0:T(8,128)(2,1)S(1)} %slice.55), channel_id=1, source_target_pairs={{0,8},{8,0},{16,24},{24,16},{1,9},{9,1},{17,25},{25,17},{2,10},{10... | collective-permute-start | bytes 159752 | tf_op jit(solution)/shard_map/ppermute | solution.py:353
  75.1 6.8 %collective-permute-start.7 = (bf16[208,128]{1,0:T(8,128)(2,1)S(1)}, bf16[208,128]{1,0:T(8,128)(2,1)S(1)}, u32[]{:S(2)}, u32[]{:S(2)}) collective-permute-start(bf16[208,128]{1,0:T(8,128)(2,1)S(1)} %slice.55), channel_id=1, source_target_pairs={{0,24},{8,16},{16,8},{24,0},{1,25},{9,17},{17,9},{25,1},{2,26},{10... | collective-permute-start | bytes 159752 | tf_op jit(solution)/shard_map/ppermute | solution.py:353
  77.5 6.4 %collective-permute-start.13 = (bf16[64,128]{1,0:T(8,128)(2,1)S(1)}, bf16[64,128]{1,0:T(8,128)(2,1)S(1)}, u32[]{:S(2)}, u32[]{:S(2)}) collective-permute-start(bf16[64,128]{1,0:T(8,128)(2,1)S(1)} %convert_element_type.92), channel_id=1, source_target_pairs={{0,16},{8,24},{16,0},{24,8},{1,17},{9,25},{17,1},{25,9},{2,18},{10... | collective-permute-start | bytes 49160 | tf_op jit(solution)/shard_map/ppermute | solution.py:353
  77.5 8.0 %collective-permute-start.12 = (bf16[64,128]{1,0:T(8,128)(2,1)S(1)}, bf16[64,128]{1,0:T(8,128)(2,1)S(1)}, u32[]{:S(2)}, u32[]{:S(2)}) collective-permute-start(bf16[64,128]{1,0:T(8,128)(2,1)S(1)} %convert_element_type.92), channel_id=1, source_target_pairs={{0,8},{8,0},{16,24},{24,16},{1,9},{9,1},{17,25},{25,17},{2,10},{10... | collective-permute-start | bytes 49160 | tf_op jit(solution)/shard_map/ppermute | solution.py:353
  79.7 5.8 %collective-permute-start.14 = (bf16[64,128]{1,0:T(8,128)(2,1)S(1)}, bf16[64,128]{1,0:T(8,128)(2,1)S(1)}, u32[]{:S(2)}, u32[]{:S(2)}) collective-permute-start(bf16[64,128]{1,0:T(8,128)(2,1)S(1)} %convert_element_type.92), channel_id=1, source_target_pairs={{0,24},{8,16},{16,8},{24,0},{1,25},{9,17},{17,9},{25,1},{2,26},{10... | collective-permute-start | bytes 49160 | tf_op jit(solution)/shard_map/ppermute | solution.py:353
  82.0 8.3 %collective-permute-start.10 = (bf16[224,128]{1,0:T(8,128)(2,1)S(1)}, bf16[224,128]{1,0:T(8,128)(2,1)S(1)}, u32[]{:S(2)}, u32[]{:S(2)}) collective-permute-start(bf16[224,128]{1,0:T(8,128)(2,1)S(1)} %pad_maximum_fusion.3), channel_id=1, source_target_pairs={{0,2},{1,3},{2,0},{3,1},{4,6},{5,7},{6,4},{7,5},{8,10},{9,11},{10,... | collective-permute-start | bytes 172040 | tf_op jit(solution)/shard_map/ppermute | solution.py:353
  83.1 7.2 %collective-permute-start.9 = (bf16[224,128]{1,0:T(8,128)(2,1)S(1)}, bf16[224,128]{1,0:T(8,128)(2,1)S(1)}, u32[]{:S(2)}, u32[]{:S(2)}) collective-permute-start(bf16[224,128]{1,0:T(8,128)(2,1)S(1)} %pad_maximum_fusion.3), channel_id=1, source_target_pairs={{0,4},{1,5},{2,6},{3,7},{4,0},{5,1},{6,2},{7,3},{8,12},{9,13},{10,... | collective-permute-start | bytes 172040 | tf_op jit(solution)/shard_map/ppermute | solution.py:353
  84.0 6.3 %collective-permute-start.8 = (bf16[224,128]{1,0:T(8,128)(2,1)S(1)}, bf16[224,128]{1,0:T(8,128)(2,1)S(1)}, u32[]{:S(2)}, u32[]{:S(2)}) collective-permute-start(bf16[224,128]{1,0:T(8,128)(2,1)S(1)} %pad_maximum_fusion.3), channel_id=1, source_target_pairs={{0,6},{1,7},{2,4},{3,5},{4,2},{5,3},{6,0},{7,1},{8,14},{9,15},{10,... | collective-permute-start | bytes 172040 | tf_op jit(solution)/shard_map/ppermute | solution.py:353
  85.6 9.2 %collective-permute-start.16 = (bf16[64,128]{1,0:T(8,128)(2,1)S(1)}, bf16[64,128]{1,0:T(8,128)(2,1)S(1)}, u32[]{:S(2)}, u32[]{:S(2)}) collective-permute-start(bf16[64,128]{1,0:T(8,128)(2,1)S(1)} %add_convert_fusion.1), channel_id=1, source_target_pairs={{0,0},{1,1},{2,8},{3,9},{4,16},{5,17},{6,24},{7,25},{8,2},{9,3},{1... | collective-permute-start | bytes 49160 | tf_op jit(solution)/shard_map/ppermute | solution.py:443
  90.2 6.8 %collective-permute-start.15 = (bf16[64,128]{1,0:T(8,128)(2,1)S(1)}, bf16[64,128]{1,0:T(8,128)(2,1)S(1)}, u32[]{:S(2)}, u32[]{:S(2)}) collective-permute-start(bf16[64,128]{1,0:T(8,128)(2,1)S(1)} %add_convert_fusion.1), channel_id=1, source_target_pairs={{0,1},{1,0},{2,9},{3,8},{4,17},{5,16},{6,25},{7,24},{8,3},{9,2},{1... | collective-permute-start | bytes 49160 | tf_op jit(solution)/shard_map/ppermute | solution.py:443
  90.4 6.6 %collective-permute-start.11 = (bf16[4,224,128]{2,1,0:T(8,128)(2,1)S(1)}, bf16[4,224,128]{2,1,0:T(8,128)(2,1)S(1)}, u32[]{:S(2)}, u32[]{:S(2)}) collective-permute-start(bf16[4,224,128]{2,1,0:T(8,128)(2,1)S(1)} %pad_maximum_fusion.1), channel_id=1, source_target_pairs={{0,1},{1,0},{2,3},{3,2},{4,5},{5,4},{6,7},{7,6},{8,9},{9,8},{10,11... | collective-permute-start | bytes 688136 | tf_op jit(solution)/shard_map/ppermute | solution.py:353
  97.2 2.5 %copy-start.1 = (bf16[48,256]{1,0:T(8,128)(2,1)S(1)}, bf16[48,256]{1,0:T(8,128)(2,1)}, u32[]{:S(2)}) copy-start(bf16[48,256]{1,0:T(8,128)(2,1)} %param.16) | copy-start | bytes 73732

commit v3 on v2

v3 whole, which is shorter than its diff:
```python
import functools

import jax
import jax.numpy as jnp
from jax import lax
from jax.experimental import pallas as pl
from jax.experimental.pallas import tpu as pltpu
from jax.sharding import PartitionSpec as P

TILE = 32
LANES = 128
BLOCK_ROWS = 32
CHUNK = 256
VMEM_LIMIT = 48 << 20
F32 = jnp.float32
BF16 = jnp.bfloat16


def dot(left_op, right_op, left_dim=1, right_dim=0):
    return lax.dot_general(
        left_op,
        right_op,
        (((left_dim,), (right_dim,)), ((), ())),
        preferred_element_type=F32,
    )


def norm(field):
    centred = field - jnp.mean(field, axis=0, keepdims=True)
    scaling = lax.rsqrt(jnp.mean(centred * centred, axis=0, keepdims=True) + 1e-05)
    return centred * scaling, scaling


def forward(inputs, in_turned, out_turned, act_ref, slope_ref, hidden_ref):
    hid = out_turned.shape[1]
    result = None
    for j in range(0, hid, CHUNK):
        half_gate = dot(in_turned[j : j + CHUNK, :], inputs).astype(BF16)
        up = dot(in_turned[hid + j : hid + j + CHUNK, :], inputs).astype(BF16)
        twice_sig = 1.0 + jnp.tanh(half_gate)
        act = half_gate * twice_sig
        hidden = act * up
        act_ref[j : j + CHUNK, :] = act
        slope_ref[j : j + CHUNK, :] = up * (twice_sig + act * (2.0 - twice_sig))
        if hidden_ref is not None:
            hidden_ref[j : j + CHUNK, :] = hidden
        part = dot(out_turned[:, j : j + CHUNK], hidden)
        result = part if result is None else result + part
    return result


def backward(grad_out, normed, scaling, gain, w_in, w_out, act_ref, slope_ref, both_ref):
    hid = w_out.shape[0]
    grad_normed = None
    for j in range(0, hid, CHUNK):
        grad_hidden = dot(w_out[j : j + CHUNK, :], grad_out).astype(BF16)
        grad_gate = grad_hidden * slope_ref[j : j + CHUNK, :]
        grad_up = grad_hidden * act_ref[j : j + CHUNK, :]
        if both_ref is not None:
            both_ref[j : j + CHUNK, :] = grad_gate
            both_ref[hid + j : hid + j + CHUNK, :] = grad_up
        part = dot(w_in[:, j : j + CHUNK], grad_gate)
        part = part + dot(w_in[:, hid + j : hid + j + CHUNK], grad_up)
        grad_normed = part if grad_normed is None else grad_normed + part
    grad_normed = grad_normed * gain
    mean = jnp.mean(grad_normed, axis=0, keepdims=True)
    slant = jnp.mean(grad_normed * normed, axis=0, keepdims=True)
    return scaling * (grad_normed - mean - normed * slant)


def turned(x):
    return jnp.transpose(x.astype(F32)).astype(x.dtype)


def prepare_kernel(
    counts_ref,
    order_ref,
    bins_ref,
    perm_ref,
    gain_first_ref,
    first_in_ref,
    first_out_ref,
    gain_second_ref,
    second_in_ref,
    second_out_ref,
    head_ref,
    first_half,
    first_in_turned,
    first_out_turned,
    second_half,
    second_in_turned,
    second_out_turned,
    head_turned,
    gains_ref,
    live_ref,
    target_ref,
    tile_ref,
    rows_ref,
):
    cols, rows = bins_ref.shape
    hid = first_out_ref.shape[0]
    group = LANES // cols
    row_index, col_index = lax.axis_index("row"), lax.axis_index("col")
    for half, half_turned, whole in (
        (first_half, first_in_turned, first_in_ref),
        (second_half, second_in_turned, second_in_ref),
    ):
        half[:, :hid] = whole[:, :hid] * jnp.asarray(0.5, BF16)
        half[:, hid:] = whole[:, hid:]
        half_turned[...] = turned(half[...])
    first_out_turned[...] = turned(first_out_ref[...])
    second_out_turned[...] = turned(second_out_ref[...])
    head_turned[...] = turned(head_ref[...])
    gains_ref[:, 0:1] = jnp.transpose(gain_first_ref[...])
    gains_ref[:, 1:2] = jnp.transpose(gain_second_ref[...])

    count = counts_ref[0, col_index]

    def place(t, carry):
        tile_ref[order_ref[0, t]] = jnp.where(t < count, 1.0, 0.0).astype(F32)
        return carry

    lax.fori_loop(0, order_ref.shape[1], place, 0, unroll=8)
    lane_tile = lax.broadcasted_iota(jnp.int32, (1, LANES), 1) // TILE
    tiles = LANES // TILE
    for k in range(live_ref.shape[0]):
        part = jnp.full((1, LANES), tile_ref[k * tiles], F32)
        for t in range(1, tiles):
            part = jnp.where(lane_tile == t, tile_ref[k * tiles + t], part)
        live_ref[k : k + 1, :] = part

    perm_rows = perm_ref[pl.ds(row_index, 1), :] - row_index * rows
    perm_line = perm_ref[pl.ds(col_index // (rows // cols), 1), :] - col_index * cols
    perm_cols = perm_line[:, :cols]
    for k in range(1, rows // cols):
        other = perm_line[:, k * cols : (k + 1) * cols]
        perm_cols = jnp.where(lax.rem(col_index, rows // cols) == k, other, perm_cols)
    pick_rows = (lax.broadcasted_iota(jnp.int32, (rows, rows), 0) == perm_rows).astype(BF16)
    pick_cols = (lax.broadcasted_iota(jnp.int32, (cols, cols), 0) == perm_cols).astype(BF16)
    bins = bins_ref[...].astype(F32).astype(BF16)
    moved = dot(pick_rows, bins, 0, 1).astype(BF16)
    rows_ref[...] = dot(moved, pick_cols)
    target_ref[...] = jnp.concatenate(
        [rows_ref[pl.ds(k, rows // group, stride=group), :] for k in range(group)], axis=1
    )


def prepare(
    counts,
    order,
    bins,
    perm,
    gain_first,
    first_in,
    first_out,
    gain_second,
    second_in,
    second_out,
    head,
):
    cols, rows = bins.shape
    width, double = first_in.shape
    hid = first_out.shape[0]
    lines = rows * cols // LANES
    shapes = [
        ((width, double), BF16),
        ((double, width), BF16),
        ((width, hid), BF16),
        ((width, double), BF16),
        ((double, width), BF16),
        ((width, hid), BF16),
        ((width, head.shape[0]), BF16),
        ((width, 2), F32),
        ((lines, LANES), F32),
        ((lines, LANES), F32),
    ]
    smem, vmem = pl.BlockSpec(memory_space=pltpu.SMEM), pl.BlockSpec(memory_space=pltpu.VMEM)
    return pl.pallas_call(
        prepare_kernel,
        in_specs=[smem, smem] + [vmem] * 9,
        out_specs=[vmem] * len(shapes),
        out_shape=[jax.ShapeDtypeStruct(shape, dtype) for shape, dtype in shapes],
        scratch_shapes=[
            pltpu.SMEM((rows * cols // TILE,), F32),
            pltpu.VMEM((rows, cols), F32),
        ],
        compiler_params=pltpu.CompilerParams(vmem_limit_bytes=16 << 20),
        cost_estimate=pl.CostEstimate(
            flops=1 << 30, bytes_accessed=4 << 20, transcendentals=0
        ),
    )(
        counts,
        order,
        bins,
        perm,
        gain_first,
        first_in,
        first_out,
        gain_second,
        second_in,
        second_out,
        head,
    )


def pair_kernel(
    tokens,
    pair_ref,
    left_ref,
    right_ref,
    first_out_ref,
    second_out_ref,
    head_turned,
    first_half,
    first_in_turned,
    first_out_turned,
    second_half,
    second_in_turned,
    second_out_turned,
    head_ref,
    gains_ref,
    live_ref,
    target_ref,
    pair_grad_ref,
    buffer_ref,
    right_grad_ref,
    act_one,
    slope_one,
    act_two,
    slope_two,
    hidden_two,
    both_two,
    in_sum,
    out_sum,
    head_sum,
    right_sum,
):
    block_rows, cols, width = pair_ref.shape
    pairs = block_rows * cols
    hid = first_out_ref.shape[0]
    step = pl.program_id(0)
    vectors = pairs // LANES
    blocks, depth, _ = buffer_ref.shape
    own_rows = pl.num_programs(0) * block_rows // blocks
    share = depth - max(own_rows, 16)

    @pl.when(step == 0)
    def _():
        right_sum[...] = jnp.zeros_like(right_sum)
        in_sum[...] = jnp.zeros_like(in_sum)
        out_sum[...] = jnp.zeros_like(out_sum)
        head_sum[...] = jnp.zeros_like(head_sum)
        buffer_ref[...] = jnp.zeros_like(buffer_ref)

    field = pair_ref[...].astype(F32) + left_ref[:, :width][:, None, :]
    field = (field + right_ref[...].astype(F32)[None]).reshape(pairs, width)
    field = jnp.transpose(field)
    normed_one, scaling_one = norm(field)
    inputs_one = (normed_one * gains_ref[:, 0:1]).astype(BF16)
    delta_one = forward(inputs_one, first_in_turned, first_out_turned, act_one, slope_one, None)
    pair_one = (field + delta_one).astype(BF16).astype(F32)

    normed_two, scaling_two = norm(pair_one)
    inputs_two = (normed_two * gains_ref[:, 1:2]).astype(BF16)
    delta_two = forward(
        inputs_two, second_in_turned, second_out_turned, act_two, slope_two, hidden_two
    )
    live = jnp.concatenate(
        [live_ref[pl.ds(step * vectors + k, 1), :] for k in range(vectors)], axis=1
    )
    pair_two = (pair_one + live * delta_two).astype(BF16)

    logits = dot(head_turned[...], pair_two)
    exponent = jnp.exp(logits - jnp.max(logits, axis=0, keepdims=True))
    probability = exponent * (1.0 / jnp.sum(exponent, axis=0, keepdims=True))
    target = jnp.concatenate(
        [target_ref[pl.ds(step * vectors + k, 1), :] for k in range(vectors)], axis=1
    ).astype(jnp.int32)
    onehot = lax.broadcasted_iota(jnp.int32, logits.shape, 0) == target
    grad_logits = (probability - onehot.astype(F32)).astype(BF16)
    grad_two = dot(head_ref[...], grad_logits).astype(BF16).astype(F32)
    head_sum[...] += dot(grad_logits, pair_two, 1, 1)

    grad_delta = (grad_two * live).astype(BF16)
    back_two = backward(
        grad_delta,
        normed_two,
        scaling_two,
        gains_ref[:, 1:2],
        second_half,
        second_out_ref,
        act_two,
        slope_two,
        both_two,
    )
    in_sum[...] += dot(inputs_two, both_two[...], 1, 1)
    out_sum[...] += dot(grad_delta, hidden_two[...], 1, 1)

    grad_one = (grad_two + back_two).astype(BF16)
    back_one = backward(
        grad_one,
        normed_one,
        scaling_one,
        gains_ref[:, 0:1],
        first_half,
        first_out_ref,
        act_one,
        slope_one,
        None,
    )
    grad_zero = jnp.transpose(grad_one.astype(F32) + back_one).reshape(block_rows, cols, width)
    pair_grad_ref[...] = grad_zero.astype(BF16)
    right_sum[...] += jnp.sum(grad_zero, axis=0)
    left_grad = jnp.sum(grad_zero, axis=1).astype(BF16)
    per_step = block_rows // own_rows
    for k in range(per_step):
        part = left_grad[k * own_rows : (k + 1) * own_rows]
        buffer_ref[step * per_step + k, share : share + own_rows, :] = part

    @pl.when(step == pl.num_programs(0) - 1)
    def _():
        scale = 1.0 / tokens
        right_grad_ref[...] = right_sum[...].astype(BF16)
        parts = []
        for j in range(0, 2 * hid, width):
            factor = scale * 0.5 if j < hid else scale
            parts.append((in_sum[:, j : j + width] * factor).astype(BF16))
        for j in range(0, hid, width):
            parts.append((jnp.transpose(out_sum[:, j : j + width]) * scale).astype(BF16))
        parts.append((head_sum[...] * scale).astype(BF16))
        first = 0
        for part in parts:
            for block, offset, start, stop in pieces(first, part.shape[0], share):
                buffer_ref[block, offset : offset + stop - start, :] = part[start:stop]
            first += part.shape[0]


def pieces(first, count, share):
    found, at = [], first
    while at < first + count:
        stop = min(first + count, (at // share + 1) * share)
        found.append((at // share, at % share, at - first, stop - first))
        at = stop
    return found


def unpack_kernel(share, gathered_ref, proj_ref, in_ref, out_ref, head_ref, single_ref):
    width, double = in_ref.shape
    cols = gathered_ref.shape[1] - share
    blocks = gathered_ref.shape[0]
    rows = single_ref.shape[1]
    own_rows = rows // blocks
    cols -= max(own_rows, 16)

    def put(first, count, ref, row, col):
        for block, offset, start, stop in pieces(first, count, share):
            part = gathered_ref[block, offset : offset + stop - start, :].astype(F32)
            ref[row + start : row + stop, col : col + width] = part

    for j in range(0, double, width):
        put(j, width, in_ref, 0, j)
    put(double, out_ref.shape[0], out_ref, 0, 0)
    put(double + out_ref.shape[0], head_ref.shape[0], head_ref, 0, 0)
    at = share + cols
    left = jnp.concatenate(
        [gathered_ref[b, at : at + own_rows, :].astype(F32) for b in range(blocks)], axis=0
    ).astype(BF16)
    ratio = rows // cols
    first = lax.axis_index("row") * ratio
    right = jnp.concatenate(
        [gathered_ref[first + k, share : share + cols, :] for k in range(ratio)], axis=0
    )
    single = dot(proj_ref[:, :width], left, 1, 1)
    single_ref[...] = single + dot(proj_ref[:, width:], right, 1, 1)


def unpack(gathered, proj_weight, hid, bins, rows, share):
    width = gathered.shape[2]
    shapes = [(width, 2 * hid), (hid, width), (bins, width), (proj_weight.shape[0], rows)]
    vmem = pl.BlockSpec(memory_space=pltpu.VMEM)
    return pl.pallas_call(
        functools.partial(unpack_kernel, share),
        in_specs=[vmem, vmem],
        out_specs=[vmem] * 4,
        out_shape=[jax.ShapeDtypeStruct(shape, F32) for shape in shapes],
        compiler_params=pltpu.CompilerParams(vmem_limit_bytes=16 << 20),
    )(gathered, proj_weight)


def pair_grid(
    pair_in,
    projected,
    right_part,
    first_out,
    second_out,
    head_turned,
    prepared,
    tokens,
    n_col,
    share,
):
    rows, cols, width = pair_in.shape
    block_rows = min(BLOCK_ROWS, rows)
    pairs = block_rows * cols
    hid = first_out.shape[0]
    bins = head_turned.shape[0]
    depth = share + max(rows // n_col, 16)

    def whole(x):
        return pl.BlockSpec(x.shape, lambda i: (0,) * x.ndim)

    def fixed(*shape):
        return pl.BlockSpec(shape, lambda i: (0,) * len(shape))

    small = (right_part, first_out, second_out, head_turned, *prepared)
    macs = rows * cols * width * (16 * hid + 3 * bins)
    return pl.pallas_call(
        functools.partial(pair_kernel, tokens),
        grid=(rows // block_rows,),
        in_specs=[
            pl.BlockSpec((block_rows, cols, width), lambda i: (i, 0, 0)),
            pl.BlockSpec((block_rows, projected.shape[1]), lambda i: (i, 0)),
        ]
        + [whole(x) for x in small],
        out_specs=[
            pl.BlockSpec((block_rows, cols, width), lambda i: (i, 0, 0)),
            fixed(n_col, depth, width),
            fixed(cols, width),
        ],
        scratch_shapes=[
            pltpu.VMEM((hid, pairs), BF16),
            pltpu.VMEM((hid, pairs), BF16),
            pltpu.VMEM((hid, pairs), BF16),
            pltpu.VMEM((hid, pairs), BF16),
            pltpu.VMEM((hid, pairs), BF16),
            pltpu.VMEM((2 * hid, pairs), BF16),
            pltpu.VMEM((width, 2 * hid), F32),
            pltpu.VMEM((width, hid), F32),
            pltpu.VMEM((bins, width), F32),
            pltpu.VMEM((cols, width), F32),
        ],
        out_shape=[
            jax.ShapeDtypeStruct((rows, cols, width), BF16),
            jax.ShapeDtypeStruct((n_col, depth, width), BF16),
            jax.ShapeDtypeStruct((cols, width), BF16),
        ],
        compiler_params=pltpu.CompilerParams(
            vmem_limit_bytes=VMEM_LIMIT, dimension_semantics=("arbitrary",)
        ),
        cost_estimate=pl.CostEstimate(
            flops=2 * macs,
            bytes_accessed=4 * rows * cols * width,
            transcendentals=2 * rows * cols * hid,
        ),
    )(pair_in, projected, *small)


def swap(x, axis, size, mask):
    return lax.ppermute(x, axis, [(i, i ^ mask) for i in range(size)])


def tree_sum(parts):
    parts = [p.astype(F32) for p in parts]
    while len(parts) > 1:
        parts = [parts[k] + parts[k + 1] for k in range(0, len(parts), 2)]
    return parts[0]


def local(
    n_row,
    n_col,
    singles,
    pair_in,
    proj_weight,
    gain_first,
    first_in,
    first_out,
    gain_second,
    second_in,
    second_out,
    head_weight,
    pae_bins,
    chain_perm,
    resolved_counts,
    tile_order,
):
    rows, cols, width = pair_in.shape
    tokens = chain_perm.shape[0]
    hid = first_out.shape[0]
    bins = head_weight.shape[1]
    col_index = lax.axis_index("col")
    ratio = rows // cols

    joined = jnp.concatenate([singles.T, proj_weight], axis=1)
    joined = lax.all_gather(joined, "col", axis=0, tiled=True)
    projected = dot(joined[:, :rows], joined[:, rows:], 0, 0)
    own_half = lax.dynamic_slice_in_dim(
        projected[:, width:], (col_index % ratio) * cols, cols, 0
    ).astype(BF16)
    right_part = lax.ppermute(
        own_half,
        ("row", "col"),
        [
            ((c // ratio) * n_col + z * ratio + c % ratio, z * n_col + c)
            for z in range(n_row)
            for c in range(n_col)
        ],
    )
    head_turned = head_weight.T
    prepared = prepare(
        resolved_counts,
        tile_order,
        pae_bins.T,
        chain_perm.reshape(n_row, rows),
        gain_first.reshape(1, width),
        first_in,
        first_out,
        gain_second.reshape(1, width),
        second_in,
        second_out,
        head_turned,
    )

    share = -(-(3 * hid + bins) // (n_col * 16)) * 16
    pair_grad, buffer, right_grad = pair_grid(
        pair_in,
        projected,
        right_part,
        first_out,
        second_out,
        head_turned,
        prepared,
        tokens,
        n_col,
        share,
    )

    buffer = lax.all_to_all(buffer, "col", 0, 0, tiled=True)
    buffer = tree_sum([buffer[k] for k in range(n_col)]).astype(BF16)
    own = jnp.concatenate([buffer[:share], right_grad], axis=0)
    own = tree_sum([own] + [swap(own, "row", n_row, k) for k in range(1, n_row)]).astype(BF16)
    own = jnp.concatenate([own, buffer[share:]], axis=0)
    gathered = lax.all_gather(own, "col", axis=0)
    in_grad, out_grad, head_grad, single_grad = unpack(
        gathered, proj_weight, hid, bins, rows, share
    )
    return pair_grad, single_grad.T, in_grad, out_grad, head_grad.T


def solution(mesh):
    in_specs = (
        P("row", "col"),
        P("row", "col", None),
        P("col", None),
        P(),
        P(),
        P(),
        P(),
        P(),
        P(),
        P(),
        P("row", "col"),
        P(),
        P("row", None),
        P("row", "col"),
    )
    out_specs = (P("row", "col", None), P("row", "col"), P(), P(), P())
    return jax.shard_map(
        functools.partial(local, mesh.shape["row"], mesh.shape["col"]),
        mesh=mesh,
        in_specs=in_specs,
        out_specs=out_specs,
        check_vma=False,
    )
```

time: 101 us -> 97.5 us (0.965)
  the two profiles are of different devices: /device:TPU:6 before, /device:TPU:0 now
where the time goes in v3:
time: 97.5 us; the launch traced here: 96.9 us
  Pallas kernels  39.9 us (41%)
  blocking collectives  37.4 us (38%)
  local copies, waits for them, and re-layouts  8.54 us (9%)
  starting transfers between devices  5.25 us (5%)
  waiting for transfers between devices  3.87 us (4%)
    pallas_call x1, Pallas kernels, pair_grid(): pl.pallas_call(functools.partial(pair_kernel, tokens), grid=(rows // bloc...  37 us
    all_to_all x1, blocking collectives, local(): buffer = lax.all_to_all(buffer, 'col', 0, 0, tiled=True)  17.5 us
    all_gather x1, blocking collectives, local(): joined = lax.all_gather(joined, 'col', axis=0, tiled=True)  10.9 us
    all_gather x1, blocking collectives, local(): gathered = lax.all_gather(own, 'col', axis=0)  9.07 us
    unnamed x32, local copies, waits for them, and re-layouts  8.52 us
    ppermute x3, starting transfers between devices, swap(): return lax.ppermute(x, axis, [(i, i ^ mask) for i in range(size)])  4.45 us
    ppermute x3, waiting for transfers between devices, swap(): return lax.ppermute(x, axis, [(i, i ^ mask) for i in range(size)])  3.86 us
    pallas_call x1, Pallas kernels, prepare(): pl.pallas_call(prepare_kernel, in_specs=[smem, smem] + [vmem] * 9, out_sp...  1.97 us
  transfers between devices with their start and end apart: 4, of which 1 were waited for; matrix products, arithmetic and copies ran while one was open for 0% of the time, Pallas kernels for 2%

profile of v3, /device:TPU:0, one launch (start us, length us, event | category | flops | bytes accessed | tf_op | source)
XLA Modules:
  0.0 96.9 jit_solution(15392816663294622191)
XLA Ops:
  0.6 0.7 pad_maximum_fusion.2
  1.4 10.9 %all_gather.9 = bf16[384,384]{1,0:T(8,128)(2,1)S(1)} all-gather(bf16[48,384]{1,0:T(8,128)(2,1)S(1)} %pad_maximum_fusion.2), channel_id=1, replica_groups=mesh['row'=4,'col'=8] {'col'}, dimensions={0}, use_global_device_ids=true | all-gather | bytes 331776 | tf_op jit(solution)/shard_map/all_gather | solution.py:495
  12.3 0.0 copy-start.5
  12.3 0.0 copy-start.7
  12.3 0.2 fusion.left_ref
  12.5 0.0 copy-start.1
  12.6 0.8 collective-permute-start
  13.4 0.0 copy-start.2
  13.4 0.9 copy-done.2
  14.3 0.0 copy-start.3
  14.3 0.9 copy-done.3
  15.3 0.0 copy-start.4
  15.3 0.9 copy-done.4
  16.2 0.0 copy-start.6
  16.2 0.9 copy-done.6
  17.1 0.0 copy-start.8
  17.1 0.8 copy-done.8
  17.8 0.0 copy-start.9
  17.8 0.7 copy-done.9
  18.5 0.0 copy-start.11
  18.6 0.7 copy-done.11
  19.2 0.0 copy-start.12
  19.2 0.7 copy-done.12
  19.9 0.0 copy-start.13
  19.9 0.7 copy-done.13
  20.6 0.0 copy-start.14
  20.6 0.7 copy-done.14
  21.2 0.0 copy-start.15
  21.2 0.7 copy-done.15
  21.9 2.0 %shard_map.173 = (bf16[128,1024]{1,0:T(8,128)(2,1)S(1)}, bf16[1024,128]{1,0:T(8,128)(2,1)S(1)}, bf16[128,512]{1,0:T(8,128)(2,1)S(1)}, bf16[128,1024]{1,0:T(8,128...) custom-call(s32[1,8]{1,0:T(1,128)S(1)} %copy-done.13, ...), custom_call_target="tpu_custom_call" | custom-call | flops 1073741824 | bytes 4194304 | tf_op jit(solution)/shard_map/pallas_call | solution.py:178
  23.8 0.0 collective-permute-done.right_ref
  23.9 0.0 copy-done.5
  23.9 0.0 copy-done.7
  23.9 0.0 copy-done.10
  23.9 0.0 copy-done.1
  23.9 37.0 %shard_map.174 = (bf16[128,64,128]{2,1,0:T(8,128)(2,1)}, bf16[8,224,128]{2,1,0:T(8,128)(2,1)S(1)}, bf16[64,128]{1,0:T(8,128)(2,1)S(1)}) custom-call(bf16[128,64,128]{2,1,0:T(8,128)(2,1)S(1)} %copy-done.1, f32[128,256]{1,0:T(8,128)S(1)} %fusion.left_ref, bf16[64,128]{1,0:T(8,128)(2,1)S(1)} %collective-permute-done.right_ref, bf16[512,128]{1,0:T(8,128)(2,1)S(1)} %copy-done.5, ...), custom_call_target="tpu_custom_call" | custom-call | flops 17582522368 | bytes 4194304 | tf_op jit(solution)/shard_map/pallas_call | solution.py:417
  60.9 0.0 copy-start
  60.9 17.5 %all_to_all.5 = bf16[8,224,128]{2,1,0:T(8,128)(2,1)S(1)} all-to-all(bf16[8,224,128]{2,1,0:T(8,128)(2,1)S(1)} %get-tuple-element.33), channel_id=1, replica_groups=mesh['row'=4,'col'=8] {'col'}, dimensions={0} | all-to-all | bytes 917504 | tf_op jit(solution)/shard_map/all_to_all | solution.py:538
  78.4 0.1 add_convert_fusion.1
  78.5 0.7 collective-permute-start.2
  79.1 0.1 collective-permute-start.1
  79.2 3.7 %collective-permute-start.3 = (bf16[272,128]{1,0:T(8,128)(2,1)S(1)}, bf16[272,128]{1,0:T(8,128)(2,1)S(1)}, u32[]{:S(2)}, u32[]{:S(2)}) collective-permute-start(bf16[272,128]{1,0:T(8,128)(2,1)S(1)} %pad_maximum_fusion.1), channel_id=1, source_target_pairs={{0,24},{8,16},{16,8},{24,0},{1,25},{9,17},{17,9},{25,1},{2,26},{10... | collective-permute-start | bytes 208904 | tf_op jit(solution)/shard_map/ppermute | solution.py:459
  82.9 3.9 %collective-permute-done.2 = bf16[272,128]{1,0:T(8,128)(2,1)S(1)} collective-permute-done((bf16[272,128]{1,0:T(8,128)(2,1)S(1)}, bf16[272,128]{1,0:T(8,128)(2,1)S(1)}, u32[]{:S(2)}, u32[]{:S(2)}) %collective-permute-start.2) | collective-permute-done | bytes 69664 | tf_op jit(solution)/shard_map/ppermute | solution.py:459
  86.8 0.0 collective-permute-done.1
  86.8 0.0 collective-permute-done.3
  86.8 9.1 %all-gather = bf16[2304,128]{1,0:T(8,128)(2,1)S(1)} all-gather(bf16[288,128]{1,0:T(8,128)(2,1)S(1)} %pad_maximum_fusion), channel_id=2, replica_groups=mesh['row'=4,'col'=8] {'col'}, dimensions={0}, use_global_device_ids=true | all-gather | bytes 663552 | tf_op jit(solution)/shard_map/all_gather | solution.py:543
  95.9 0.0 copy-done
  95.9 0.9 shard_map.175
  (8 shorter events, 0.1 us)
Async XLA Ops:
  12.3 11.6 %copy-start.5 = (bf16[512,128]{1,0:T(8,128)(2,1)S(1)}, bf16[512,128]{1,0:T(8,128)(2,1)}, u32[]{:S(2)}) copy-start(bf16[512,128]{1,0:T(8,128)(2,1)} %first_out_ref.3) | copy-start | bytes 393220
  12.3 11.6 %copy-start.7 = (bf16[512,128]{1,0:T(8,128)(2,1)S(1)}, bf16[512,128]{1,0:T(8,128)(2,1)}, u32[]{:S(2)}) copy-start(bf16[512,128]{1,0:T(8,128)(2,1)} %second_out_ref.3) | copy-start | bytes 393220
  12.3 11.6 %copy-start.10 = (bf16[128,64]{0,1:T(8,128)(2,1)S(1)}, bf16[128,64]{0,1:T(8,128)(2,1)}, u32[]{:S(2)}) copy-start(bf16[128,64]{0,1:T(8,128)(2,1)} %param.23) | copy-start | bytes 49156
  12.5 11.4 %copy-start.1 = (bf16[128,64,128]{2,1,0:T(8,128)(2,1)S(1)}, bf16[128,64,128]{2,1,0:T(8,128)(2,1)}, u32[]{:S(2)}) copy-start(bf16[128,64,128]{2,1,0:T(8,128)(2,1)} %pair_ref.1) | copy-start | bytes 6291460
  12.6 11.3 %collective-permute-start = (bf16[64,128]{1,0:T(8,128)(2,1)S(1)}, bf16[64,128]{1,0:T(8,128)(2,1)S(1)}, u32[]{:S(2)}, u32[]{:S(2)}) collective-permute-start(bf16[64,128]{1,0:T(8,128)(2,1)S(1)} %dynamic-slice_convert_fusion), channel_id=1, source_target_pairs={{0,0},{1,1},{8,2},{9,3},{16,4},{17,5},{24,6},{25,7},{2,8},{3,9},{1... | collective-permute-start | bytes 49160 | tf_op jit(solution)/shard_map/ppermute | solution.py:500
  13.4 1.0 copy-start.2
  14.3 0.9 copy-start.3
  15.3 0.9 copy-start.4
  16.2 0.9 copy-start.6
  17.1 0.8 copy-start.8
  17.8 0.7 copy-start.9
  18.5 0.7 copy-start.11
  19.2 0.7 copy-start.12
  19.9 0.7 copy-start.13
  20.6 0.7 copy-start.14
  21.2 0.7 copy-start.15
  60.9 35.0 %copy-start = (bf16[48,256]{1,0:T(8,128)(2,1)S(1)}, bf16[48,256]{1,0:T(8,128)(2,1)}, u32[]{:S(2)}) copy-start(bf16[48,256]{1,0:T(8,128)(2,1)} %proj_ref.1) | copy-start | bytes 73732
  78.5 8.3 %collective-permute-start.2 = (bf16[272,128]{1,0:T(8,128)(2,1)S(1)}, bf16[272,128]{1,0:T(8,128)(2,1)S(1)}, u32[]{:S(2)}, u32[]{:S(2)}) collective-permute-start(bf16[272,128]{1,0:T(8,128)(2,1)S(1)} %pad_maximum_fusion.1), channel_id=1, source_target_pairs={{0,16},{8,24},{16,0},{24,8},{1,17},{9,25},{17,1},{25,9},{2,18},{10... | collective-permute-start | bytes 208904 | tf_op jit(solution)/shard_map/ppermute | solution.py:459
  79.1 7.7 %collective-permute-start.1 = (bf16[272,128]{1,0:T(8,128)(2,1)S(1)}, bf16[272,128]{1,0:T(8,128)(2,1)S(1)}, u32[]{:S(2)}, u32[]{:S(2)}) collective-permute-start(bf16[272,128]{1,0:T(8,128)(2,1)S(1)} %pad_maximum_fusion.1), channel_id=1, source_target_pairs={{0,8},{8,0},{16,24},{24,16},{1,9},{9,1},{17,25},{25,17},{2,10},{10... | collective-permute-start | bytes 208904 | tf_op jit(solution)/shard_map/ppermute | solution.py:459
  79.2 7.6 %collective-permute-start.3 = (bf16[272,128]{1,0:T(8,128)(2,1)S(1)}, bf16[272,128]{1,0:T(8,128)(2,1)S(1)}, u32[]{:S(2)}, u32[]{:S(2)}) collective-permute-start(bf16[272,128]{1,0:T(8,128)(2,1)S(1)} %pad_maximum_fusion.1), channel_id=1, source_target_pairs={{0,24},{8,16},{16,8},{24,0},{1,25},{9,17},{17,9},{25,1},{2,26},{10... | collective-permute-start | bytes 208904 | tf_op jit(solution)/shard_map/ppermute | solution.py:459

commit v4 on v3

--- a/solution.py
+++ b/solution.py
@@ -11,7 +11,9 @@
 LANES = 128
 BLOCK_ROWS = 32
 CHUNK = 256
-VMEM_LIMIT = 48 << 20
+VMEM_LIMIT = 61 << 20
+PARTS = 2
+AHEAD = 2
 F32 = jnp.float32
 BF16 = jnp.bfloat16
 
@@ -31,34 +33,38 @@
     return centred * scaling, scaling
 
 
-def forward(inputs, in_turned, out_turned, act_ref, slope_ref, hidden_ref):
+def forward(inputs, in_turned, out_turned, act_ref, slope_ref, hidden_ref, lanes):
     hid = out_turned.shape[1]
     result = None
     for j in range(0, hid, CHUNK):
         half_gate = dot(in_turned[j : j + CHUNK, :], inputs).astype(BF16)
         up = dot(in_turned[hid + j : hid + j + CHUNK, :], inputs).astype(BF16)
+        yield
         twice_sig = 1.0 + jnp.tanh(half_gate)
         act = half_gate * twice_sig
         hidden = act * up
-        act_ref[j : j + CHUNK, :] = act
-        slope_ref[j : j + CHUNK, :] = up * (twice_sig + act * (2.0 - twice_sig))
+        act_ref[j : j + CHUNK, lanes] = act
+        slope_ref[j : j + CHUNK, lanes] = up * (twice_sig + act * (2.0 - twice_sig))
         if hidden_ref is not None:
-            hidden_ref[j : j + CHUNK, :] = hidden
+            hidden_ref[j : j + CHUNK, lanes] = hidden
+        yield
         part = dot(out_turned[:, j : j + CHUNK], hidden)
         result = part if result is None else result + part
     return result
 
 
-def backward(grad_out, normed, scaling, gain, w_in, w_out, act_ref, slope_ref, both_ref):
+def backward(grad_out, normed, scaling, gain, w_in, w_out, act_ref, slope_ref, both_ref, lanes):
     hid = w_out.shape[0]
     grad_normed = None
     for j in range(0, hid, CHUNK):
         grad_hidden = dot(w_out[j : j + CHUNK, :], grad_out).astype(BF16)
-        grad_gate = grad_hidden * slope_ref[j : j + CHUNK, :]
-        grad_up = grad_hidden * act_ref[j : j + CHUNK, :]
+        yield
+        grad_gate = grad_hidden * slope_ref[j : j + CHUNK, lanes]
+        grad_up = grad_hidden * act_ref[j : j + CHUNK, lanes]
         if both_ref is not None:
-            both_ref[j : j + CHUNK, :] = grad_gate
-            both_ref[hid + j : hid + j + CHUNK, :] = grad_up
+            both_ref[j : j + CHUNK, lanes] = grad_gate
+            both_ref[hid + j : hid + j + CHUNK, lanes] = grad_up
+        yield
         part = dot(w_in[:, j : j + CHUNK], grad_gate)
         part = part + dot(w_in[:, hid + j : hid + j + CHUNK], grad_up)
         grad_normed = part if grad_normed is None else grad_normed + part
@@ -174,23 +180,7 @@
         ((lines, LANES), F32),
         ((lines, LANES), F32),
     ]
-    smem, vmem = pl.BlockSpec(memory_space=pltpu.SMEM), pl.BlockSpec(memory_space=pltpu.VMEM)
-    return pl.pallas_call(
-        prepare_kernel,
-        in_specs=[smem, smem] + [vmem] * 9,
-        out_specs=[vmem] * len(shapes),
-        out_shape=[jax.ShapeDtypeStruct(shape, dtype) for shape, dtype in shapes],
-        scratch_shapes=[
-            pltpu.SMEM((rows * cols // TILE,), F32),
-            pltpu.VMEM((rows, cols), F32),
-        ],
-        compiler_params=pltpu.CompilerParams(vmem_limit_bytes=16 << 20),
-        cost_estimate=pl.CostEstimate(
-            flops=1 << 30, bytes_accessed=4 << 20, transcendentals=0
-        ),
-    )(
-        counts,
-        order,
+    small = (
         bins,
         perm,
         gain_first,
@@ -201,6 +191,24 @@
         second_out,
         head,
     )
+    return pl.pallas_call(
+        prepare_kernel,
+        grid_spec=pltpu.PrefetchScalarGridSpec(
+            num_scalar_prefetch=2,
+            grid=(1,),
+            in_specs=[pl.BlockSpec(x.shape, lambda i, *_: (0, 0)) for x in small],
+            out_specs=[pl.BlockSpec(shape, lambda i, *_: (0, 0)) for shape, _ in shapes],
+            scratch_shapes=[
+                pltpu.SMEM((rows * cols // TILE,), F32),
+                pltpu.VMEM((rows, cols), F32),
+            ],
+        ),
+        out_shape=[jax.ShapeDtypeStruct(shape, dtype) for shape, dtype in shapes],
+        compiler_params=pltpu.CompilerParams(vmem_limit_bytes=VMEM_LIMIT),
+        cost_estimate=pl.CostEstimate(
+            flops=1 << 30, bytes_accessed=4 << 20, transcendentals=0
+        ),
+    )(counts, order, *small)
 
 
 def pair_kernel(
@@ -252,70 +260,102 @@
         head_sum[...] = jnp.zeros_like(head_sum)
         buffer_ref[...] = jnp.zeros_like(buffer_ref)
 
-    field = pair_ref[...].astype(F32) + left_ref[:, :width][:, None, :]
-    field = (field + right_ref[...].astype(F32)[None]).reshape(pairs, width)
-    field = jnp.transpose(field)
-    normed_one, scaling_one = norm(field)
-    inputs_one = (normed_one * gains_ref[:, 0:1]).astype(BF16)
-    delta_one = forward(inputs_one, first_in_turned, first_out_turned, act_one, slope_one, None)
-    pair_one = (field + delta_one).astype(BF16).astype(F32)
-
-    normed_two, scaling_two = norm(pair_one)
-    inputs_two = (normed_two * gains_ref[:, 1:2]).astype(BF16)
-    delta_two = forward(
-        inputs_two, second_in_turned, second_out_turned, act_two, slope_two, hidden_two
-    )
-    live = jnp.concatenate(
-        [live_ref[pl.ds(step * vectors + k, 1), :] for k in range(vectors)], axis=1
-    )
-    pair_two = (pair_one + live * delta_two).astype(BF16)
-
-    logits = dot(head_turned[...], pair_two)
-    exponent = jnp.exp(logits - jnp.max(logits, axis=0, keepdims=True))
-    probability = exponent * (1.0 / jnp.sum(exponent, axis=0, keepdims=True))
-    target = jnp.concatenate(
-        [target_ref[pl.ds(step * vectors + k, 1), :] for k in range(vectors)], axis=1
-    ).astype(jnp.int32)
-    onehot = lax.broadcasted_iota(jnp.int32, logits.shape, 0) == target
-    grad_logits = (probability - onehot.astype(F32)).astype(BF16)
-    grad_two = dot(head_ref[...], grad_logits).astype(BF16).astype(F32)
-    head_sum[...] += dot(grad_logits, pair_two, 1, 1)
-
-    grad_delta = (grad_two * live).astype(BF16)
-    back_two = backward(
-        grad_delta,
-        normed_two,
-        scaling_two,
-        gains_ref[:, 1:2],
-        second_half,
-        second_out_ref,
-        act_two,
-        slope_two,
-        both_two,
-    )
-    in_sum[...] += dot(inputs_two, both_two[...], 1, 1)
-    out_sum[...] += dot(grad_delta, hidden_two[...], 1, 1)
-
-    grad_one = (grad_two + back_two).astype(BF16)
-    back_one = backward(
-        grad_one,
-        normed_one,
-        scaling_one,
-        gains_ref[:, 0:1],
-        first_half,
-        first_out_ref,
-        act_one,
-        slope_one,
-        None,
-    )
-    grad_zero = jnp.transpose(grad_one.astype(F32) + back_one).reshape(block_rows, cols, width)
-    pair_grad_ref[...] = grad_zero.astype(BF16)
-    right_sum[...] += jnp.sum(grad_zero, axis=0)
-    left_grad = jnp.sum(grad_zero, axis=1).astype(BF16)
-    per_step = block_rows // own_rows
-    for k in range(per_step):
-        part = left_grad[k * own_rows : (k + 1) * own_rows]
-        buffer_ref[step * per_step + k, share : share + own_rows, :] = part
+    def flow(part_index):
+        part_pairs = pairs // PARTS
+        part_vectors = vectors // PARTS
+        lanes = slice(part_index * part_pairs, (part_index + 1) * part_pairs)
+        part_rows = slice(
+            part_index * (block_rows // PARTS), (part_index + 1) * (block_rows // PARTS)
+        )
+        field = pair_ref[part_rows].astype(F32) + left_ref[part_rows, :width][:, None, :]
+        field = (field + right_ref[...].astype(F32)[None]).reshape(part_pairs, width)
+        field = jnp.transpose(field)
+        yield
+        normed_one, scaling_one = norm(field)
+        inputs_one = (normed_one * gains_ref[:, 0:1]).astype(BF16)
+        yield
+        delta_one = yield from forward(
+            inputs_one, first_in_turned, first_out_turned, act_one, slope_one, None, lanes
+        )
+        yield
+        pair_one = (field + delta_one).astype(BF16).astype(F32)
+
+        normed_two, scaling_two = norm(pair_one)
+        inputs_two = (normed_two * gains_ref[:, 1:2]).astype(BF16)
+        yield
+        delta_two = yield from forward(
+            inputs_two, second_in_turned, second_out_turned, act_two, slope_two, hidden_two, lanes
+        )
+        yield
+        line = step * vectors + part_index * part_vectors
+        live = jnp.concatenate(
+            [live_ref[pl.ds(line + k, 1), :] for k in range(part_vectors)], axis=1
+        )
+        pair_two = (pair_one + live * delta_two).astype(BF16)
+
+        logits = dot(head_turned[...], pair_two)
+        yield
+        exponent = jnp.exp(logits - jnp.max(logits, axis=0, keepdims=True))
+        probability = exponent * (1.0 / jnp.sum(exponent, axis=0, keepdims=True))
+        target = jnp.concatenate(
+            [target_ref[pl.ds(line + k, 1), :] for k in range(part_vectors)], axis=1
+        ).astype(jnp.int32)
+        onehot = lax.broadcasted_iota(jnp.int32, logits.shape, 0) == target
+        grad_logits = (probability - onehot.astype(F32)).astype(BF16)
+        yield
+        grad_two = dot(head_ref[...], grad_logits).astype(BF16).astype(F32)
+        head_sum[...] += dot(grad_logits, pair_two, 1, 1)
+
+        grad_delta = (grad_two * live).astype(BF16)
+        yield
+        back_two = yield from backward(
+            grad_delta,
+            normed_two,
+            scaling_two,
+            gains_ref[:, 1:2],
+            second_half,
+            second_out_ref,
+            act_two,
+            slope_two,
+            both_two,
+            lanes,
+        )
+        in_sum[...] += dot(inputs_two, both_two[:, lanes], 1, 1)
+        out_sum[...] += dot(grad_delta, hidden_two[:, lanes], 1, 1)
+        yield
+
+        grad_one = (grad_two + back_two).astype(BF16)
+        back_one = yield from backward(
+            grad_one,
+            normed_one,
+            scaling_one,
+            gains_ref[:, 0:1],
+            first_half,
+            first_out_ref,
+            act_one,
+            slope_one,
+            None,
+            lanes,
+        )
+        yield
+        grad_zero = jnp.transpose(grad_one.astype(F32) + back_one).reshape(-1, cols, width)
+        pair_grad_ref[part_rows] = grad_zero.astype(BF16)
+        right_sum[...] += jnp.sum(grad_zero, axis=0)
+        left_grad = jnp.sum(grad_zero, axis=1).astype(BF16)
+        per_part = block_rows // PARTS // own_rows
+        per_step = block_rows // own_rows
+        for k in range(per_part):
+            part = left_grad[k * own_rows : (k + 1) * own_rows]
+            buffer_ref[step * per_step + part_index * per_part + k, share : share + own_rows, :] = part
+
+    flows = [flow(k) for k in range(PARTS)]
+    for k, each in enumerate(flows):
+        for _ in range((PARTS - 1 - k) * AHEAD):
+            next(each)
+    while flows:
+        for each in list(flows):
+            if next(each, flows) is flows:
+                flows.remove(each)
 
     @pl.when(step == pl.num_programs(0) - 1)
     def _():

time: 97.5 us -> 93.7 us (0.961)
  local copies, waits for them, and re-layouts: 8.54 us -> 0.62 us
  Pallas kernels: 39.9 us -> 41.4 us
  waiting for transfers between devices: 3.87 us -> 5.34 us
  other arithmetic: 0.87 us -> 2.3 us
    unnamed x32 -> x6, local copies, waits for them, and re-layouts: 8.52 us -> 0.6 us
    pallas_call x1, Pallas kernels: 1.97 us -> 3.99 us  [prepare(): pl.pallas_call(prepare_kernel, grid_spec=pltpu.PrefetchScalarGridSpec(num...]
    ppermute x3, waiting for transfers between devices: 3.86 us -> 5.34 us  [swap(): return lax.ppermute(x, axis, [(i, i ^ mask) for i in range(size)])]
  transfers between devices with their start and end apart: 4 -> 4, of which waited for: 1 -> 2; matrix products, arithmetic and copies ran while one was open for 0% -> 0% of each run, Pallas kernels for 2% -> 4%
where the time goes in v4:
time: 93.7 us; the launch traced here: 93.1 us
  Pallas kernels  41.4 us (44%)
  blocking collectives  37.5 us (40%)
  waiting for transfers between devices  5.34 us (6%)
  starting transfers between devices  5.05 us (5%)
  other arithmetic  2.3 us (2%)
    pallas_call x1, Pallas kernels, pair_grid(): pl.pallas_call(functools.partial(pair_kernel, tokens), grid=(rows // bloc...  36.5 us
    all_to_all x1, blocking collectives, local(): buffer = lax.all_to_all(buffer, 'col', 0, 0, tiled=True)  17.5 us
    all_gather x1, blocking collectives, local(): joined = lax.all_gather(joined, 'col', axis=0, tiled=True)  10.9 us
    all_gather x1, blocking collectives, local(): gathered = lax.all_gather(own, 'col', axis=0)  9.04 us
    ppermute x3, waiting for transfers between devices, swap(): return lax.ppermute(x, axis, [(i, i ^ mask) for i in range(size)])  5.34 us
    ppermute x3, starting transfers between devices, swap(): return lax.ppermute(x, axis, [(i, i ^ mask) for i in range(size)])  4.39 us
    pallas_call x1, Pallas kernels, prepare(): pl.pallas_call(prepare_kernel, grid_spec=pltpu.PrefetchScalarGridSpec(num...  3.99 us
  transfers between devices with their start and end apart: 4, of which 2 were waited for; matrix products, arithmetic and copies ran while one was open for 0% of the time, Pallas kernels for 4%

profile of v4, /device:TPU:0, one launch (start us, length us, event | category | flops | bytes accessed | tf_op | source)
XLA Modules:
  0.0 93.1 jit_solution(15662213557241620645)
XLA Ops:
  0.6 0.7 pad_maximum_fusion.2
  1.4 10.9 %all_gather.9 = bf16[384,384]{1,0:T(8,128)(2,1)S(1)} all-gather(bf16[48,384]{1,0:T(8,128)(2,1)S(1)} %pad_maximum_fusion.2), channel_id=1, replica_groups=mesh['row'=4,'col'=8] {'col'}, dimensions={0}, use_global_device_ids=true | all-gather | bytes 331776 | tf_op jit(solution)/shard_map/all_gather | solution.py:535
  12.3 0.2 fusion.left_ref
  12.5 0.0 copy-start.1
  12.5 0.7 collective-permute-start
  13.2 4.0 %shard_map.173 = (bf16[128,1024]{1,0:T(8,128)(2,1)}, bf16[1024,128]{1,0:T(8,128)(2,1)}, bf16[128,512]{1,0:T(8,128)(2,1)}, bf16[128,1024]{1,0:T(8,128)(2,1)}, bf1...) custom-call(s32[1,8]{1,0:T(1,128)} %counts_ref.1, ...), custom_call_target="tpu_custom_call" | custom-call | flops 1073741824 | bytes 4194304 | tf_op jit(solution)/shard_map/pallas_call | solution.py:194
  17.2 0.0 collective-permute-done.right_ref
  17.2 0.0 copy-start.2
  17.2 0.0 copy-done.1
  17.2 0.6 copy-done.2
  17.8 36.5 %shard_map.174 = (bf16[128,64,128]{2,1,0:T(8,128)(2,1)}, bf16[8,224,128]{2,1,0:T(8,128)(2,1)}, bf16[64,128]{1,0:T(8,128)(2,1)}) custom-call(bf16[128,64,128]{2,1,0:T(8,128)(2,1)} %pair_ref.1, f32[128,256]{1,0:T(8,128)} %copy-done.1, bf16[64,128]{1,0:T(8,128)(2,1)} %copy-done.2, bf16[512,128]{1,0:T(8,128)(2,1)} %first_out_ref.3, ...), custom_call_target="tpu_custom_call" | custom-call | flops 17582522368 | bytes 4194304 | tf_op jit(solution)/shard_map/pallas_call | solution.py:457
  54.3 0.0 copy-start
  54.3 17.5 %all_to_all.5 = bf16[8,224,128]{2,1,0:T(8,128)(2,1)S(1)} all-to-all(bf16[8,224,128]{2,1,0:T(8,128)(2,1)} %get-tuple-element.33), channel_id=1, replica_groups=mesh['row'=4,'col'=8] {'col'}, dimensions={0} | all-to-all | bytes 917504 | tf_op jit(solution)/shard_map/all_to_all | solution.py:578
  71.8 0.1 add_convert_fusion.1
  71.9 0.7 pad_maximum_fusion.1
  72.6 0.6 collective-permute-start.2
  73.2 3.0 %collective-permute-start.1 = (bf16[272,128]{1,0:T(8,128)(2,1)S(1)}, bf16[272,128]{1,0:T(8,128)(2,1)S(1)}, u32[]{:S(2)}, u32[]{:S(2)}) collective-permute-start(bf16[272,128]{1,0:T(8,128)(2,1)S(1)} %pad_maximum_fusion.1), channel_id=1, source_target_pairs={{0,8},{8,0},{16,24},{24,16},{1,9},{9,1},{17,25},{25,17},{2,10},{10... | collective-permute-start | bytes 208904 | tf_op jit(solution)/shard_map/ppermute | solution.py:499
  76.3 0.8 collective-permute-start.3
  77.0 2.2 %collective-permute-done.2 = bf16[272,128]{1,0:T(8,128)(2,1)S(1)} collective-permute-done((bf16[272,128]{1,0:T(8,128)(2,1)S(1)}, bf16[272,128]{1,0:T(8,128)(2,1)S(1)}, u32[]{:S(2)}, u32[]{:S(2)}) %collective-permute-start.2) | collective-permute-done | bytes 69664 | tf_op jit(solution)/shard_map/ppermute | solution.py:499
  79.2 0.0 collective-permute-done.1
  79.2 3.2 %collective-permute-done.3 = bf16[272,128]{1,0:T(8,128)(2,1)S(1)} collective-permute-done((bf16[272,128]{1,0:T(8,128)(2,1)S(1)}, bf16[272,128]{1,0:T(8,128)(2,1)S(1)}, u32[]{:S(2)}, u32[]{:S(2)}) %collective-permute-start.3) | collective-permute-done | bytes 69664 | tf_op jit(solution)/shard_map/ppermute | solution.py:499
  82.4 0.8 add_convert_fusion
  83.1 9.0 %all-gather = bf16[2304,128]{1,0:T(8,128)(2,1)S(1)} all-gather(bf16[288,128]{1,0:T(8,128)(2,1)S(1)} %pad_maximum_fusion), channel_id=2, replica_groups=mesh['row'=4,'col'=8] {'col'}, dimensions={0}, use_global_device_ids=true | all-gather | bytes 663552 | tf_op jit(solution)/shard_map/all_gather | solution.py:583
  92.2 0.0 copy-done
  92.2 0.9 %shard_map.175 = (f32[128,1024]{1,0:T(8,128)}, f32[512,128]{1,0:T(8,128)}, f32[64,128]{1,0:T(8,128)}, f32[48,128]{1,0:T(8,128)}) custom-call(bf16[8,288,128]{2,1,0:T(8,128)(2,1)S(1)} %bitcast.13, bf16[48,256]{1,0:T(8,128)(2,1)S(1)} %copy-done), custom_call_target="tpu_custom_call" | custom-call | tf_op jit(solution)/shard_map/pallas_call | solution.py:421
  (5 shorter events, 0.0 us)
Async XLA Ops:
  12.5 4.7 %copy-start.1 = (f32[128,256]{1,0:T(8,128)}, f32[128,256]{1,0:T(8,128)S(1)}, u32[]{:S(2)}) copy-start(f32[128,256]{1,0:T(8,128)S(1)} %fusion.left_ref) | copy-start | bytes 393220
  12.5 4.7 %collective-permute-start = (bf16[64,128]{1,0:T(8,128)(2,1)S(1)}, bf16[64,128]{1,0:T(8,128)(2,1)S(1)}, u32[]{:S(2)}, u32[]{:S(2)}) collective-permute-start(bf16[64,128]{1,0:T(8,128)(2,1)S(1)} %dynamic-slice_convert_fusion), channel_id=1, source_target_pairs={{0,0},{1,1},{8,2},{9,3},{16,4},{17,5},{24,6},{25,7},{2,8},{3,9},{1... | collective-permute-start | bytes 49160 | tf_op jit(solution)/shard_map/ppermute | solution.py:540
  17.2 0.6 copy-start.2
  54.3 37.9 %copy-start = (bf16[48,256]{1,0:T(8,128)(2,1)S(1)}, bf16[48,256]{1,0:T(8,128)(2,1)}, u32[]{:S(2)}) copy-start(bf16[48,256]{1,0:T(8,128)(2,1)} %proj_ref.1) | copy-start | bytes 73732
  72.6 6.6 %collective-permute-start.2 = (bf16[272,128]{1,0:T(8,128)(2,1)S(1)}, bf16[272,128]{1,0:T(8,128)(2,1)S(1)}, u32[]{:S(2)}, u32[]{:S(2)}) collective-permute-start(bf16[272,128]{1,0:T(8,128)(2,1)S(1)} %pad_maximum_fusion.1), channel_id=1, source_target_pairs={{0,16},{8,24},{16,0},{24,8},{1,17},{9,25},{17,1},{25,9},{2,18},{10... | collective-permute-start | bytes 208904 | tf_op jit(solution)/shard_map/ppermute | solution.py:499
  73.2 6.0 %collective-permute-start.1 = (bf16[272,128]{1,0:T(8,128)(2,1)S(1)}, bf16[272,128]{1,0:T(8,128)(2,1)S(1)}, u32[]{:S(2)}, u32[]{:S(2)}) collective-permute-start(bf16[272,128]{1,0:T(8,128)(2,1)S(1)} %pad_maximum_fusion.1), channel_id=1, source_target_pairs={{0,8},{8,0},{16,24},{24,16},{1,9},{9,1},{17,25},{25,17},{2,10},{10... | collective-permute-start | bytes 208904 | tf_op jit(solution)/shard_map/ppermute | solution.py:499
  76.3 6.1 %collective-permute-start.3 = (bf16[272,128]{1,0:T(8,128)(2,1)S(1)}, bf16[272,128]{1,0:T(8,128)(2,1)S(1)}, u32[]{:S(2)}, u32[]{:S(2)}) collective-permute-start(bf16[272,128]{1,0:T(8,128)(2,1)S(1)} %pad_maximum_fusion.1), channel_id=1, source_target_pairs={{0,24},{8,16},{16,8},{24,0},{1,25},{9,17},{17,9},{25,1},{2,26},{10... | collective-permute-start | bytes 208904 | tf_op jit(solution)/shard_map/ppermute | solution.py:499

commit v5 on v4

--- a/solution.py
+++ b/solution.py
@@ -481,8 +481,8 @@
         ],
         out_shape=[
             jax.ShapeDtypeStruct((rows, cols, width), BF16),
-            jax.ShapeDtypeStruct((n_col, depth, width), BF16),
-            jax.ShapeDtypeStruct((cols, width), BF16),
+            pltpu.VMEM((n_col, depth, width), BF16),
+            pltpu.VMEM((cols, width), BF16),
         ],
         compiler_params=pltpu.CompilerParams(
             vmem_limit_bytes=VMEM_LIMIT, dimension_semantics=("arbitrary",)

time: 93.7 us -> 91.1 us (0.972)
  other arithmetic: 2.3 us -> 0.87 us
where the time goes in v5:
time: 91.1 us; the launch traced here: 90.7 us
  Pallas kernels  41.2 us (45%)
  blocking collectives  37.3 us (41%)
  starting transfers between devices  5.11 us (6%)
  waiting for transfers between devices  4.61 us (5%)
    pallas_call x1, Pallas kernels, pair_grid(): pl.pallas_call(functools.partial(pair_kernel, tokens), grid=(rows // bloc...  36.3 us
    all_to_all x1, blocking collectives, local(): buffer = lax.all_to_all(buffer, 'col', 0, 0, tiled=True)  17.3 us
    all_gather x1, blocking collectives, local(): joined = lax.all_gather(joined, 'col', axis=0, tiled=True)  10.9 us
    all_gather x1, blocking collectives, local(): gathered = lax.all_gather(own, 'col', axis=0)  9.11 us
    ppermute x3, waiting for transfers between devices, swap(): return lax.ppermute(x, axis, [(i, i ^ mask) for i in range(size)])  4.6 us
    ppermute x3, starting transfers between devices, swap(): return lax.ppermute(x, axis, [(i, i ^ mask) for i in range(size)])  4.45 us
    pallas_call x1, Pallas kernels, prepare(): pl.pallas_call(prepare_kernel, grid_spec=pltpu.PrefetchScalarGridSpec(num...  3.99 us
  transfers between devices with their start and end apart: 4, of which 2 were waited for; matrix products, arithmetic and copies ran while one was open for 0% of the time, Pallas kernels for 4%

profile of v5, /device:TPU:0, one launch (start us, length us, event | category | flops | bytes accessed | tf_op | source)
XLA Modules:
  0.0 90.7 jit_solution(8080096424344924114)
XLA Ops:
  0.6 0.7 pad_maximum_fusion.2
  1.4 10.9 %all_gather.9 = bf16[384,384]{1,0:T(8,128)(2,1)S(1)} all-gather(bf16[48,384]{1,0:T(8,128)(2,1)S(1)} %pad_maximum_fusion.2), channel_id=1, replica_groups=mesh['row'=4,'col'=8] {'col'}, dimensions={0}, use_global_device_ids=true | all-gather | bytes 331776 | tf_op jit(solution)/shard_map/all_gather | solution.py:535
  12.3 0.2 fusion.left_ref
  12.5 0.0 copy-start.1
  12.5 0.7 collective-permute-start
  13.2 4.0 %shard_map.173 = (bf16[128,1024]{1,0:T(8,128)(2,1)}, bf16[1024,128]{1,0:T(8,128)(2,1)}, bf16[128,512]{1,0:T(8,128)(2,1)}, bf16[128,1024]{1,0:T(8,128)(2,1)}, bf1...) custom-call(s32[1,8]{1,0:T(1,128)} %counts_ref.1, ...), custom_call_target="tpu_custom_call" | custom-call | flops 1073741824 | bytes 4194304 | tf_op jit(solution)/shard_map/pallas_call | solution.py:194
  17.2 0.0 collective-permute-done.right_ref
  17.2 0.0 copy-start.2
  17.2 0.0 copy-done.1
  17.2 0.6 copy-done.2
  17.8 36.3 %shard_map.174 = (bf16[128,64,128]{2,1,0:T(8,128)(2,1)}, bf16[8,224,128]{2,1,0:T(8,128)(2,1)S(1)}, bf16[64,128]{1,0:T(8,128)(2,1)S(1)}) custom-call(bf16[128,64,128]{2,1,0:T(8,128)(2,1)} %pair_ref.1, f32[128,256]{1,0:T(8,128)} %copy-done.1, bf16[64,128]{1,0:T(8,128)(2,1)} %copy-done.2, bf16[512,128]{1,0:T(8,128)(2,1)} %first_out_ref.3, ...), custom_call_target="tpu_custom_call" | custom-call | flops 17582522368 | bytes 4194304 | tf_op jit(solution)/shard_map/pallas_call | solution.py:457
  54.1 0.0 copy-start
  54.1 17.3 %all_to_all.5 = bf16[8,224,128]{2,1,0:T(8,128)(2,1)S(1)} all-to-all(bf16[8,224,128]{2,1,0:T(8,128)(2,1)S(1)} %get-tuple-element.33), channel_id=1, replica_groups=mesh['row'=4,'col'=8] {'col'}, dimensions={0} | all-to-all | bytes 917504 | tf_op jit(solution)/shard_map/all_to_all | solution.py:578
  71.4 0.1 add_convert_fusion.1
  71.5 0.7 collective-permute-start.2
  72.2 2.3 %collective-permute-start.1 = (bf16[272,128]{1,0:T(8,128)(2,1)S(1)}, bf16[272,128]{1,0:T(8,128)(2,1)S(1)}, u32[]{:S(2)}, u32[]{:S(2)}) collective-permute-start(bf16[272,128]{1,0:T(8,128)(2,1)S(1)} %pad_maximum_fusion.1), channel_id=1, source_target_pairs={{0,8},{8,0},{16,24},{24,16},{1,9},{9,1},{17,25},{25,17},{2,10},{10... | collective-permute-start | bytes 208904 | tf_op jit(solution)/shard_map/ppermute | solution.py:499
  74.4 1.5 %collective-permute-start.3 = (bf16[272,128]{1,0:T(8,128)(2,1)S(1)}, bf16[272,128]{1,0:T(8,128)(2,1)S(1)}, u32[]{:S(2)}, u32[]{:S(2)}) collective-permute-start(bf16[272,128]{1,0:T(8,128)(2,1)S(1)} %pad_maximum_fusion.1), channel_id=1, source_target_pairs={{0,24},{8,16},{16,8},{24,0},{1,25},{9,17},{17,9},{25,1},{2,26},{10... | collective-permute-start | bytes 208904 | tf_op jit(solution)/shard_map/ppermute | solution.py:499
  76.0 3.1 %collective-permute-done.2 = bf16[272,128]{1,0:T(8,128)(2,1)S(1)} collective-permute-done((bf16[272,128]{1,0:T(8,128)(2,1)S(1)}, bf16[272,128]{1,0:T(8,128)(2,1)S(1)}, u32[]{:S(2)}, u32[]{:S(2)}) %collective-permute-start.2) | collective-permute-done | bytes 69664 | tf_op jit(solution)/shard_map/ppermute | solution.py:499
  79.1 0.0 collective-permute-done.1
  79.1 1.5 %collective-permute-done.3 = bf16[272,128]{1,0:T(8,128)(2,1)S(1)} collective-permute-done((bf16[272,128]{1,0:T(8,128)(2,1)S(1)}, bf16[272,128]{1,0:T(8,128)(2,1)S(1)}, u32[]{:S(2)}, u32[]{:S(2)}) %collective-permute-start.3) | collective-permute-done | bytes 69664 | tf_op jit(solution)/shard_map/ppermute | solution.py:499
  80.7 9.1 %all-gather = bf16[2304,128]{1,0:T(8,128)(2,1)S(1)} all-gather(bf16[288,128]{1,0:T(8,128)(2,1)S(1)} %pad_maximum_fusion), channel_id=2, replica_groups=mesh['row'=4,'col'=8] {'col'}, dimensions={0}, use_global_device_ids=true | all-gather | bytes 663552 | tf_op jit(solution)/shard_map/all_gather | solution.py:583
  89.8 0.0 copy-done
  89.8 0.9 %shard_map.175 = (f32[128,1024]{1,0:T(8,128)}, f32[512,128]{1,0:T(8,128)}, f32[64,128]{1,0:T(8,128)}, f32[48,128]{1,0:T(8,128)}) custom-call(bf16[8,288,128]{2,1,0:T(8,128)(2,1)S(1)} %bitcast.13, bf16[48,256]{1,0:T(8,128)(2,1)S(1)} %copy-done), custom_call_target="tpu_custom_call" | custom-call | tf_op jit(solution)/shard_map/pallas_call | solution.py:421
  (7 shorter events, 0.1 us)
Async XLA Ops:
  12.5 4.7 %copy-start.1 = (f32[128,256]{1,0:T(8,128)}, f32[128,256]{1,0:T(8,128)S(1)}, u32[]{:S(2)}) copy-start(f32[128,256]{1,0:T(8,128)S(1)} %fusion.left_ref) | copy-start | bytes 393220
  12.5 4.7 %collective-permute-start = (bf16[64,128]{1,0:T(8,128)(2,1)S(1)}, bf16[64,128]{1,0:T(8,128)(2,1)S(1)}, u32[]{:S(2)}, u32[]{:S(2)}) collective-permute-start(bf16[64,128]{1,0:T(8,128)(2,1)S(1)} %dynamic-slice_convert_fusion), channel_id=1, source_target_pairs={{0,0},{1,1},{8,2},{9,3},{16,4},{17,5},{24,6},{25,7},{2,8},{3,9},{1... | collective-permute-start | bytes 49160 | tf_op jit(solution)/shard_map/ppermute | solution.py:540
  17.2 0.6 copy-start.2
  54.1 35.7 %copy-start = (bf16[48,256]{1,0:T(8,128)(2,1)S(1)}, bf16[48,256]{1,0:T(8,128)(2,1)}, u32[]{:S(2)}) copy-start(bf16[48,256]{1,0:T(8,128)(2,1)} %proj_ref.1) | copy-start | bytes 73732
  71.5 7.6 %collective-permute-start.2 = (bf16[272,128]{1,0:T(8,128)(2,1)S(1)}, bf16[272,128]{1,0:T(8,128)(2,1)S(1)}, u32[]{:S(2)}, u32[]{:S(2)}) collective-permute-start(bf16[272,128]{1,0:T(8,128)(2,1)S(1)} %pad_maximum_fusion.1), channel_id=1, source_target_pairs={{0,16},{8,24},{16,0},{24,8},{1,17},{9,25},{17,1},{25,9},{2,18},{10... | collective-permute-start | bytes 208904 | tf_op jit(solution)/shard_map/ppermute | solution.py:499
  72.2 6.9 %collective-permute-start.1 = (bf16[272,128]{1,0:T(8,128)(2,1)S(1)}, bf16[272,128]{1,0:T(8,128)(2,1)S(1)}, u32[]{:S(2)}, u32[]{:S(2)}) collective-permute-start(bf16[272,128]{1,0:T(8,128)(2,1)S(1)} %pad_maximum_fusion.1), channel_id=1, source_target_pairs={{0,8},{8,0},{16,24},{24,16},{1,9},{9,1},{17,25},{25,17},{2,10},{10... | collective-permute-start | bytes 208904 | tf_op jit(solution)/shard_map/ppermute | solution.py:499
  74.4 6.2 %collective-permute-start.3 = (bf16[272,128]{1,0:T(8,128)(2,1)S(1)}, bf16[272,128]{1,0:T(8,128)(2,1)S(1)}, u32[]{:S(2)}, u32[]{:S(2)}) collective-permute-start(bf16[272,128]{1,0:T(8,128)(2,1)S(1)} %pad_maximum_fusion.1), channel_id=1, source_target_pairs={{0,24},{8,16},{16,8},{24,0},{1,25},{9,17},{17,9},{25,1},{2,26},{10... | collective-permute-start | bytes 208904 | tf_op jit(solution)/shard_map/ppermute | solution.py:499

commit v6 on v5

--- a/solution.py
+++ b/solution.py
@@ -9,7 +9,7 @@
 
 TILE = 32
 LANES = 128
-BLOCK_ROWS = 32
+BLOCK_ROWS = 64
 CHUNK = 256
 VMEM_LIMIT = 61 << 20
 PARTS = 2

time: 91.1 us -> 90.6 us (level)
  no operation moved by 1% of the time
where the time goes in v6:
time: 90.6 us; the launch traced here: 90.3 us
  Pallas kernels  40.8 us (45%)
  blocking collectives  37.3 us (41%)
  starting transfers between devices  5.11 us (6%)
  waiting for transfers between devices  4.61 us (5%)
    pallas_call x1, Pallas kernels, pair_grid(): pl.pallas_call(functools.partial(pair_kernel, tokens), grid=(rows // bloc...  35.8 us
    all_to_all x1, blocking collectives, local(): buffer = lax.all_to_all(buffer, 'col', 0, 0, tiled=True)  17.3 us
    all_gather x1, blocking collectives, local(): joined = lax.all_gather(joined, 'col', axis=0, tiled=True)  10.9 us
    all_gather x1, blocking collectives, local(): gathered = lax.all_gather(own, 'col', axis=0)  9.11 us
    ppermute x3, waiting for transfers between devices, swap(): return lax.ppermute(x, axis, [(i, i ^ mask) for i in range(size)])  4.6 us
    ppermute x3, starting transfers between devices, swap(): return lax.ppermute(x, axis, [(i, i ^ mask) for i in range(size)])  4.45 us
    pallas_call x1, Pallas kernels, prepare(): pl.pallas_call(prepare_kernel, grid_spec=pltpu.PrefetchScalarGridSpec(num...  3.99 us
  transfers between devices with their start and end apart: 4, of which 2 were waited for; matrix products, arithmetic and copies ran while one was open for 0% of the time, Pallas kernels for 4%

profile of v6, /device:TPU:0, one launch (start us, length us, event | category | flops | bytes accessed | tf_op | source)
XLA Modules:
  0.0 90.3 jit_solution(6476125275184730742)
XLA Ops:
  0.6 0.7 pad_maximum_fusion.2
  1.4 10.9 %all_gather.9 = bf16[384,384]{1,0:T(8,128)(2,1)S(1)} all-gather(bf16[48,384]{1,0:T(8,128)(2,1)S(1)} %pad_maximum_fusion.2), channel_id=1, replica_groups=mesh['row'=4,'col'=8] {'col'}, dimensions={0}, use_global_device_ids=true | all-gather | bytes 331776 | tf_op jit(solution)/shard_map/all_gather | solution.py:535
  12.3 0.2 fusion.left_ref
  12.5 0.0 copy-start.1
  12.5 0.7 collective-permute-start
  13.2 4.0 %shard_map.173 = (bf16[128,1024]{1,0:T(8,128)(2,1)}, bf16[1024,128]{1,0:T(8,128)(2,1)}, bf16[128,512]{1,0:T(8,128)(2,1)}, bf16[128,1024]{1,0:T(8,128)(2,1)}, bf1...) custom-call(s32[1,8]{1,0:T(1,128)} %counts_ref.1, ...), custom_call_target="tpu_custom_call" | custom-call | flops 1073741824 | bytes 4194304 | tf_op jit(solution)/shard_map/pallas_call | solution.py:194
  17.2 0.0 collective-permute-done.right_ref
  17.2 0.0 copy-start.2
  17.2 0.0 copy-done.1
  17.2 0.6 copy-done.2
  17.8 35.8 %shard_map.174 = (bf16[128,64,128]{2,1,0:T(8,128)(2,1)}, bf16[8,224,128]{2,1,0:T(8,128)(2,1)S(1)}, bf16[64,128]{1,0:T(8,128)(2,1)S(1)}) custom-call(bf16[128,64,128]{2,1,0:T(8,128)(2,1)} %pair_ref.1, f32[128,256]{1,0:T(8,128)} %copy-done.1, bf16[64,128]{1,0:T(8,128)(2,1)} %copy-done.2, bf16[512,128]{1,0:T(8,128)(2,1)} %first_out_ref.3, ...), custom_call_target="tpu_custom_call" | custom-call | flops 17582522368 | bytes 4194304 | tf_op jit(solution)/shard_map/pallas_call | solution.py:457
  53.7 0.0 copy-start
  53.7 17.3 %all_to_all.5 = bf16[8,224,128]{2,1,0:T(8,128)(2,1)S(1)} all-to-all(bf16[8,224,128]{2,1,0:T(8,128)(2,1)S(1)} %get-tuple-element.33), channel_id=1, replica_groups=mesh['row'=4,'col'=8] {'col'}, dimensions={0} | all-to-all | bytes 917504 | tf_op jit(solution)/shard_map/all_to_all | solution.py:578
  71.0 0.1 add_convert_fusion.1
  71.1 0.7 collective-permute-start.2
  71.7 2.3 %collective-permute-start.1 = (bf16[272,128]{1,0:T(8,128)(2,1)S(1)}, bf16[272,128]{1,0:T(8,128)(2,1)S(1)}, u32[]{:S(2)}, u32[]{:S(2)}) collective-permute-start(bf16[272,128]{1,0:T(8,128)(2,1)S(1)} %pad_maximum_fusion.1), channel_id=1, source_target_pairs={{0,8},{8,0},{16,24},{24,16},{1,9},{9,1},{17,25},{25,17},{2,10},{10... | collective-permute-start | bytes 208904 | tf_op jit(solution)/shard_map/ppermute | solution.py:499
  74.0 1.5 %collective-permute-start.3 = (bf16[272,128]{1,0:T(8,128)(2,1)S(1)}, bf16[272,128]{1,0:T(8,128)(2,1)S(1)}, u32[]{:S(2)}, u32[]{:S(2)}) collective-permute-start(bf16[272,128]{1,0:T(8,128)(2,1)S(1)} %pad_maximum_fusion.1), channel_id=1, source_target_pairs={{0,24},{8,16},{16,8},{24,0},{1,25},{9,17},{17,9},{25,1},{2,26},{10... | collective-permute-start | bytes 208904 | tf_op jit(solution)/shard_map/ppermute | solution.py:499
  75.5 3.1 %collective-permute-done.2 = bf16[272,128]{1,0:T(8,128)(2,1)S(1)} collective-permute-done((bf16[272,128]{1,0:T(8,128)(2,1)S(1)}, bf16[272,128]{1,0:T(8,128)(2,1)S(1)}, u32[]{:S(2)}, u32[]{:S(2)}) %collective-permute-start.2) | collective-permute-done | bytes 69664 | tf_op jit(solution)/shard_map/ppermute | solution.py:499
  78.7 0.0 collective-permute-done.1
  78.7 1.5 %collective-permute-done.3 = bf16[272,128]{1,0:T(8,128)(2,1)S(1)} collective-permute-done((bf16[272,128]{1,0:T(8,128)(2,1)S(1)}, bf16[272,128]{1,0:T(8,128)(2,1)S(1)}, u32[]{:S(2)}, u32[]{:S(2)}) %collective-permute-start.3) | collective-permute-done | bytes 69664 | tf_op jit(solution)/shard_map/ppermute | solution.py:499
  80.2 9.1 %all-gather = bf16[2304,128]{1,0:T(8,128)(2,1)S(1)} all-gather(bf16[288,128]{1,0:T(8,128)(2,1)S(1)} %pad_maximum_fusion), channel_id=2, replica_groups=mesh['row'=4,'col'=8] {'col'}, dimensions={0}, use_global_device_ids=true | all-gather | bytes 663552 | tf_op jit(solution)/shard_map/all_gather | solution.py:583
  89.3 0.0 copy-done
  89.3 0.9 %shard_map.175 = (f32[128,1024]{1,0:T(8,128)}, f32[512,128]{1,0:T(8,128)}, f32[64,128]{1,0:T(8,128)}, f32[48,128]{1,0:T(8,128)}) custom-call(bf16[8,288,128]{2,1,0:T(8,128)(2,1)S(1)} %bitcast.13, bf16[48,256]{1,0:T(8,128)(2,1)S(1)} %copy-done), custom_call_target="tpu_custom_call" | custom-call | tf_op jit(solution)/shard_map/pallas_call | solution.py:421
  (7 shorter events, 0.1 us)
Async XLA Ops:
  12.5 4.7 %copy-start.1 = (f32[128,256]{1,0:T(8,128)}, f32[128,256]{1,0:T(8,128)S(1)}, u32[]{:S(2)}) copy-start(f32[128,256]{1,0:T(8,128)S(1)} %fusion.left_ref) | copy-start | bytes 393220
  12.5 4.7 %collective-permute-start = (bf16[64,128]{1,0:T(8,128)(2,1)S(1)}, bf16[64,128]{1,0:T(8,128)(2,1)S(1)}, u32[]{:S(2)}, u32[]{:S(2)}) collective-permute-start(bf16[64,128]{1,0:T(8,128)(2,1)S(1)} %dynamic-slice_convert_fusion), channel_id=1, source_target_pairs={{0,0},{1,1},{8,2},{9,3},{16,4},{17,5},{24,6},{25,7},{2,8},{3,9},{1... | collective-permute-start | bytes 49160 | tf_op jit(solution)/shard_map/ppermute | solution.py:540
  17.2 0.6 copy-start.2
  53.7 35.7 %copy-start = (bf16[48,256]{1,0:T(8,128)(2,1)S(1)}, bf16[48,256]{1,0:T(8,128)(2,1)}, u32[]{:S(2)}) copy-start(bf16[48,256]{1,0:T(8,128)(2,1)} %proj_ref.1) | copy-start | bytes 73732
  71.1 7.6 %collective-permute-start.2 = (bf16[272,128]{1,0:T(8,128)(2,1)S(1)}, bf16[272,128]{1,0:T(8,128)(2,1)S(1)}, u32[]{:S(2)}, u32[]{:S(2)}) collective-permute-start(bf16[272,128]{1,0:T(8,128)(2,1)S(1)} %pad_maximum_fusion.1), channel_id=1, source_target_pairs={{0,16},{8,24},{16,0},{24,8},{1,17},{9,25},{17,1},{25,9},{2,18},{10... | collective-permute-start | bytes 208904 | tf_op jit(solution)/shard_map/ppermute | solution.py:499
  71.7 6.9 %collective-permute-start.1 = (bf16[272,128]{1,0:T(8,128)(2,1)S(1)}, bf16[272,128]{1,0:T(8,128)(2,1)S(1)}, u32[]{:S(2)}, u32[]{:S(2)}) collective-permute-start(bf16[272,128]{1,0:T(8,128)(2,1)S(1)} %pad_maximum_fusion.1), channel_id=1, source_target_pairs={{0,8},{8,0},{16,24},{24,16},{1,9},{9,1},{17,25},{25,17},{2,10},{10... | collective-permute-start | bytes 208904 | tf_op jit(solution)/shard_map/ppermute | solution.py:499
  74.0 6.2 %collective-permute-start.3 = (bf16[272,128]{1,0:T(8,128)(2,1)S(1)}, bf16[272,128]{1,0:T(8,128)(2,1)S(1)}, u32[]{:S(2)}, u32[]{:S(2)}) collective-permute-start(bf16[272,128]{1,0:T(8,128)(2,1)S(1)} %pad_maximum_fusion.1), channel_id=1, source_target_pairs={{0,24},{8,16},{16,8},{24,0},{1,25},{9,17},{17,9},{25,1},{2,26},{10... | collective-permute-start | bytes 208904 | tf_op jit(solution)/shard_map/ppermute | solution.py:499
